TPU v7x, 128 devices: a whole 4x4x4 slice. The times are simulated.
128 devices in a mesh: dp: 8 (over x_lo, z), vocab: 16 (over y, x_hi, core).
Axes of the slice: x: 4 (x_hi: 2, x_lo: 2; x = x_hi * 2 + x_lo), y: 4, z: 4, core: 2. Of those that a mesh axis runs over, the one named last changes fastest.
Arguments:
- student_hidden: bfloat16 [512, 5120], P('dp'), may hold values from -64 to 64
- student_weight: bfloat16 [81920, 5120], P(('dp', 'vocab')), may hold values from -12 to 12
- teacher_hidden: bfloat16 [512, 4096], P('dp'), may hold values from -64 to 64
- teacher_weight: bfloat16 [81920, 4096], P(('dp', 'vocab')), may hold values from -12 to 12
- token_ids: int32 [512], replicated, may hold values from 0 to 81919
- group_ids: int32 [512], replicated, may hold values from 0 to 15, never falling along the last dimension, each value on 1 to 64 neighbouring positions
- response_mask: int32 [512], replicated, may hold values 0 or 1
Outputs:
- kl_tok: float32 [512], P('dp')
- logp_tok: float32 [512], P('dp')
- grad_hidden: bfloat16 [512, 5120], P('dp')
- grad_weight: bfloat16 [81920, 5120], P(('dp', 'vocab'))
All inputs are finite; a program needn't handle non-finite values.
Results may differ from a plain program's by a relative error of at most 0.006.
Values may be sent and summed in bfloat16 or wider, within the bound.
No kernel may reach another device: no remote copies, remote signals or barrier semaphores. Data moves between devices by JAX's collectives and lax.ppermute only.
A program may use at most 128 MiB of HBM per device.

v0:
```python
import jax
import jax.numpy as jnp
from jax import lax
from jax.sharding import PartitionSpec as P

SPAN = 32


def shards(
    student_hidden,
    student_weight,
    teacher_hidden,
    teacher_weight,
    token_ids,
    group_ids,
    response_mask,
):
    own_rows = student_hidden.shape[0]
    head_rows = student_weight.shape[0]
    hidden_all = lax.all_gather(student_hidden, "dp", axis=0, tiled=True)
    student_logits = jnp.einsum(
        "td,vd->tv", hidden_all, student_weight, preferred_element_type=jnp.float32
    )
    teacher_logits = jnp.einsum(
        "td,vd->tv",
        lax.all_gather(teacher_hidden, "dp", axis=0, tiled=True),
        teacher_weight,
        preferred_element_type=jnp.float32,
    )
    device_index = lax.axis_index(("dp", "vocab"))
    column = lax.broadcasted_iota(jnp.int32, (1, head_rows), 1) + device_index * head_rows
    chosen = token_ids[:, None] == column
    picked_local = jnp.sum(jnp.where(chosen, student_logits, 0.0), axis=1)
    spread = teacher_logits - student_logits
    top_s, top_t = lax.pmax(
        (jnp.max(student_logits, axis=1), jnp.max(teacher_logits, axis=1)), ("dp", "vocab")
    )
    exp_t = jnp.exp(teacher_logits - top_t[:, None])
    local_s = jnp.sum(jnp.exp(student_logits - top_s[:, None]), axis=1)
    total_s, total_t, cross, picked = lax.psum(
        (local_s, jnp.sum(exp_t, axis=1), jnp.sum(exp_t * spread, axis=1), picked_local),
        ("dp", "vocab"),
    )
    log_total_s = top_s + jnp.log(total_s)
    log_total_t = top_t + jnp.log(total_t)
    kl_all = cross / total_t - log_total_t + log_total_s
    logp_all = picked - log_total_s
    same_group = group_ids[:, None] == group_ids[None, :]
    lengths = jnp.sum(same_group.astype(jnp.float32), axis=1)
    token_weight = response_mask.astype(jnp.float32) * SPAN / lengths
    prob_s = jnp.exp(student_logits - log_total_s[:, None])
    prob_t = jnp.exp(teacher_logits - log_total_t[:, None])
    grad_logits = (token_weight[:, None] * (prob_s - prob_t)).astype(jnp.bfloat16)
    grad_weight = jnp.einsum(
        "tv,td->vd", grad_logits, hidden_all, preferred_element_type=jnp.float32
    ).astype(jnp.bfloat16)
    share = lax.psum_scatter(
        jnp.dot(grad_logits, student_weight, preferred_element_type=jnp.float32),
        ("dp", "vocab"),
        scatter_dimension=0,
        tiled=True,
    )
    grad_hidden = lax.all_gather(share.astype(jnp.bfloat16), "vocab", axis=0, tiled=True)
    first_row = lax.axis_index("dp") * own_rows
    kl_tok = lax.dynamic_slice_in_dim(kl_all, first_row, own_rows, 0)
    logp_tok = lax.dynamic_slice_in_dim(logp_all, first_row, own_rows, 0)
    return (kl_tok, logp_tok, grad_hidden, grad_weight)


def solution(mesh):
    in_specs = (
        P("dp", None),
        P(("dp", "vocab"), None),
        P("dp", None),
        P(("dp", "vocab"), None),
        P(),
        P(),
        P(),
    )
    out_specs = (P("dp"), P("dp"), P("dp", None), P(("dp", "vocab"), None))
    return jax.shard_map(shards, mesh=mesh, in_specs=in_specs, out_specs=out_specs, check_vma=False)
```

profile of v0, /device:TPU:1, one launch (start us, length us, event | category | flops | bytes accessed | tf_op | source)
XLA Modules:
  0.0 435.7 jit_solution(9584106394295851033)
XLA Ops:
  7.2 0.0 all-gather.4.cloned.1.call-start
  7.2 0.7 all-gather.4.cloned.1.call-update
  7.9 0.0 all-gather.6.cloned.1.call-start
  7.9 0.7 all-gather.6.cloned.1.call-update
  8.7 1.0 convert_reduce_fusion
  9.7 0.7 multiply_divide_fusion
  10.4 55.3 %all-gather.4.cloned.1.call-done = bf16[512,4096]{1,0:T(8,128)(2,1)} async-done(((bf16[64,4096]{1,0:T(8,128)(2,1)}), bf16[512,4096]{1,0:T(8,128)(2,1)}) %all-gather.4.cloned.1.call-update) | async-done | bytes 4194320 | tf_op jit(solution)/shard_map/all_gather | solution.py:26
  65.7 6.9 %fusion.4 = (f32[512]{0:T(512)S(1)}, f32[512,640]{1,0:T(8,128)S(1)}) fusion(bf16[512,4096]{1,0:T(8,128)(2,1)} %all-gather.4.cloned.1.call-done, bf16[640,4096]{1,0:T(8,128)(2,1)} %param.10), kind=kOutput, calls=%fused_computation.17 | convolution fusion | flops 2684681728 | bytes 10749952 | tf_op jit(solution)/shard_map/td,vd->tv/dot_general | solution.py:24
  72.6 0.0 copy-start
  72.7 56.0 %all-gather.6.cloned.1.call-done = bf16[512,5120]{1,0:T(8,128)(2,1)} async-done(((bf16[64,5120]{1,0:T(8,128)(2,1)}), bf16[512,5120]{1,0:T(8,128)(2,1)}) %all-gather.6.cloned.1.call-update) | async-done | bytes 5242896 | tf_op jit(solution)/shard_map/all_gather | solution.py:20
  128.6 8.3 %fusion.3 = (f32[512]{0:T(512)S(1)}, f32[512,640]{1,0:T(8,128)S(1)}) fusion(bf16[512,5120]{1,0:T(8,128)(2,1)} %all-gather.6.cloned.1.call-done, bf16[640,5120]{1,0:T(8,128)(2,1)} %param.8), kind=kOutput, calls=%fused_computation.16 | convolution fusion | flops 3355770368 | bytes 13109248 | tf_op jit(solution)/shard_map/td,vd->tv/dot_general | solution.py:21
  136.9 64.3 %all-reduce.3 = (f32[512]{0:T(512)S(1)}, f32[512]{0:T(512)S(1)}) all-reduce(f32[512]{0:T(512)S(1)} %get-tuple-element.19, f32[512]{0:T(512)S(1)} %get-tuple-element.21), channel_id=1, replica_groups=mesh['dp'=8,'vocab'=16] {'dp','vocab'}, use_global_device_ids=true, to_apply=%region_7.8 | all-reduce | flops 1024 | bytes 8192 | tf_op jit(solution)/shard_map/pmax | solution.py:35
  201.2 0.0 copy-done
  201.2 1.0 select_reduce_fusion
  202.2 63.8 %all-reduce.2 = (f32[512]{0:T(512)S(1)}, f32[512]{0:T(512)S(1)}) all-reduce(f32[512]{0:T(512)S(1)} %get-tuple-element.7, f32[512]{0:T(512)S(1)} %get-tuple-element.8), channel_id=1, replica_groups=mesh['dp'=8,'vocab'=16] {'dp','vocab'}, use_global_device_ids=true, to_apply=%region_9.10 | all-reduce | flops 1024 | bytes 8192 | tf_op jit(solution)/shard_map/psum | solution.py:40
  266.1 0.5 multiply_convert_fusion
  266.5 9.7 %fusion.5 = f32[512,5120]{1,0:T(8,128)} fusion(bf16[512,640]{1,0:T(8,128)(2,1)S(1)} %multiply_convert_fusion, bf16[640,5120]{1,0:T(8,128)(2,1)} %param.8), kind=kOutput, calls=%fused_computation.18 | convolution fusion | flops 3355443200 | bytes 17694720 | tf_op jit(solution)/shard_map/dot_general | solution.py:58
  276.3 114.0 %all-reduce.5 = (f32[512]{0:T(512)S(1)}, f32[512]{0:T(512)S(1)}, bf16[512,5120]{1,0:T(8,128)(2,1)}) all-reduce(f32[512]{0:T(512)S(1)} %get-tuple-element.9, f32[512]{0:T(512)S(1)} %get-tuple-element.6, f32[512,5120]{1,0:T(8,128)} %fusion.5), channel_id=1, replica_groups=mesh['dp'=8,'vocab'=16] {'dp','vocab'}, use_global_device_ids=true, to_apply=%region_3.4 | all-reduce | flops 2622464 | bytes 15736832 | tf_op jit(solution)/shard_map/psum | solution.py:40
  390.3 0.9 fusion.1
  391.2 26.6 %all-gather = bf16[16,4,5120]{2,1,0:T(4,128)(2,1)S(1)} all-gather(bf16[1,4,5120]{2,1,0:T(4,128)(2,1)S(1)} %fusion.1), channel_id=1, replica_groups=mesh['dp'=8,'vocab'=16] {'vocab'}, dimensions={0}, use_global_device_ids=true | all-gather | bytes 696320 | tf_op jit(solution)/shard_map/all_gather | solution.py:63
  417.8 1.0 reshape.22
  418.8 0.6 dynamic_slice.7
  419.3 0.6 dynamic_slice.6
  419.9 8.9 %convolution_convert_fusion = bf16[640,5120]{1,0:T(8,128)(2,1)} fusion(bf16[512,640]{1,0:T(8,128)(2,1)S(1)} %multiply_convert_fusion, bf16[512,5120]{1,0:T(8,128)(2,1)} %all-gather.6.cloned.1.call-done), kind=kOutput, calls=%fused_computation | convolution fusion | flops 3358720000 | bytes 12451840 | tf_op jit(solution)/shard_map/tv,td->vd/dot_general | solution.py:54
  (3 shorter events, 0.0 us)
Async XLA Ops:
  7.2 58.5 %all-gather.4.cloned.1.call-start = ((), (), s32[]{:S(2)}) async-start(), calls=%async_computation | async-start | bytes 4718592 | tf_op jit(solution)/shard_map/all_gather | solution.py:26
  7.9 120.7 %all-gather.6.cloned.1.call-start = ((), (), s32[]{:S(2)}) async-start(), calls=%async_computation.1 | async-start | bytes 5898240 | tf_op jit(solution)/shard_map/all_gather | solution.py:20
  72.6 128.6 %copy-start = (s32[512]{0:T(512)S(1)}, s32[512]{0:T(512)}, u32[]{:S(2)}) copy-start(s32[512]{0:T(512)} %param.11) | copy-start | bytes 6148
Sparse Core Ops, SparseCore 0:
  9.6 55.9 all-gather.3
  67.3 61.2 all-gather.5
where the time goes:
time: 436 us
  blocking collectives  269 us (62%)
  waiting for transfers between devices  113 us (26%)
  matrix products  33.9 us (8%)
  between operations  14.1 us (3%)
    psum x2, blocking collectives, shards(): lax.psum((local_s, jnp.sum(exp_t, axis=1), jnp.sum(exp_t * spread, axis=1...  178 us
    pmax x1, blocking collectives, shards(): lax.pmax((jnp.max(student_logits, axis=1), jnp.max(teacher_logits, axis=1...  64.3 us
    all_gather x1, waiting for transfers between devices, shards(): hidden_all = lax.all_gather(student_hidden, 'dp', axis=0, tiled=True)  56 us
    all_gather x1, waiting for transfers between devices, shards(): lax.all_gather(teacher_hidden, 'dp', axis=0, tiled=True)  55.3 us
    all_gather x1, blocking collectives, shards(): lax.all_gather(share.astype(jnp.bfloat16), 'vocab', axis=0, tiled=True)  26.6 us
    dot_general x1, matrix products, shards(): jnp.dot(grad_logits, student_weight, preferred_element_type=jnp.float32)  9.73 us
    dot_general x1, matrix products, shards(): jnp.einsum('tv,td->vd', grad_logits, hidden_all, preferred_element_type=j...  8.89 us
  transfers between devices with their start and end apart: 2, of which 2 were waited for; matrix products, arithmetic and copies ran while one was open for 2% of the time, Pallas kernels for 0%

commit v1 on v0

v1 whole, which is shorter than its diff:
```python
import functools

import jax
import jax.numpy as jnp
from jax import lax
from jax.experimental import pallas as pl
from jax.experimental.pallas import tpu as pltpu
from jax.sharding import PartitionSpec as P

SPAN = 32
BOTH = ("dp", "vocab")
F32 = jnp.float32
BF16 = jnp.bfloat16
I32 = jnp.int32
VMEM_BYTES = 63 * 1024 * 1024


def coordinates(device):
    dp, vocab = divmod(device, 16)
    x_lo, z = divmod(dp, 4)
    y, rest = divmod(vocab, 4)
    x_hi, core = divmod(rest, 2)
    return x_hi * 2 + x_lo, y, z, core


def device_at(x, y, z, core):
    x_hi, x_lo = divmod(x % 4, 2)
    return (x_lo * 4 + z % 4) * 16 + (y % 4) * 4 + x_hi * 2 + core


def permutation(move):
    return [(i, device_at(*move(*coordinates(i)))) for i in range(128)]


def way(core):
    return 1 - 2 * core


ALONG_Z = permutation(lambda x, y, z, c: (x, y, z + way(c), c))
ALONG_X = permutation(lambda x, y, z, c: (x + way(c), y, z, c))
ALONG_Y = permutation(lambda x, y, z, c: (x, y + way(c), z, c))
OTHER_CORE = permutation(lambda x, y, z, c: (x, y, z, 1 - c))
SAME_TOKENS = [[dp * 16 + v * 2 + c for v in range(8)] for dp in range(8) for c in range(2)]
SAME_CORE = [[i for i in range(128) if i % 2 == c] for c in range(2)]


def send(value, where):
    return lax.ppermute(value, BOTH, where)


def after(done, then):
    both = lax.optimization_barrier((done, then))
    return both


def swap(blocks):
    return [send(block, OTHER_CORE) for block in blocks]


def gather_tokens(kept, weight_columns):
    near_z, near_x, weight_columns = lax.optimization_barrier((send(kept, ALONG_Z), send(kept, ALONG_X), weight_columns))
    second = [send(near_z, ALONG_X), send(near_z, ALONG_Z), send(near_z, ALONG_Y)] + swap([near_z, near_x])
    near_zx, far_z, rest_z, o_near_z, o_near_x = lax.optimization_barrier(second)
    third = [send(far_z, ALONG_X), send(near_zx, ALONG_Y)] + swap([near_zx, far_z, rest_z])
    far_zx, rest_zx, o_near_zx, o_far_z, o_rest_z = lax.optimization_barrier(third)
    o_rest_zx, o_far_zx, weight_columns = lax.optimization_barrier((*swap([rest_zx, far_zx]), weight_columns))
    mine = [near_z, rest_z, near_x, far_z, near_zx, rest_zx, far_zx]
    theirs = [o_near_z, o_rest_z, o_near_x, o_far_z, o_near_zx, o_rest_zx, o_far_zx]
    return mine + theirs, send(weight_columns, OTHER_CORE)


def first_rows(core, odd, x_lo, z, half):
    def block(xl, zz):
        return (xl * 4 + jnp.remainder(zz, 4)) * 2

    def arrived(c):
        s = 1 - 2 * c
        k = c + odd - 2 * c * odd
        return [
            block(x_lo, z - s) + k,
            block(x_lo, z - s) + 1 - k,
            block(1 - x_lo, z) + k,
            block(x_lo, z + 2) + k,
            block(1 - x_lo, z - s) + k,
            block(1 - x_lo, z - s) + 1 - k,
            block(1 - x_lo, z + 2) + k,
        ]

    return [half * b for b in [block(x_lo, z)] + arrived(core) + arrived(1 - core)]


def start_all(copies):
    for copy in copies:
        copy.start()
    return copies


def wait_all(copies):
    for copy in copies:
        copy.wait()


def half_kernel(scalars, student, teacher, out, here, sems):
    half, width = out.shape[0], student.shape[1]
    rows = pl.ds(pl.multiple_of(scalars[0] * half, half), half)
    loads = [
        pltpu.make_async_copy(student.at[rows], here.at[:, pl.ds(0, width)], sems.at[0]),
        pltpu.make_async_copy(teacher.at[rows], here.at[:, pl.ds(width, teacher.shape[1])], sems.at[1]),
    ]
    wait_all(start_all(loads))
    store = pltpu.make_async_copy(here, out, sems.at[2])
    store.start()
    store.wait()


def place(scalars, own, blocks, columns, hidden, half, sems):
    copies = []
    for i, block in enumerate([own] + [b.at[:, columns] for b in blocks]):
        rows = pl.ds(pl.multiple_of(scalars[i], half), own.shape[0] if i == 0 else half)
        copies.append(pltpu.make_async_copy(block, hidden.at[rows], sems.at[i]))
    return start_all(copies)


def rows_product(weight, hidden, out, at):
    out[at] = lax.dot_general(weight[at], hidden[...], (((1,), (1,)), ((), ())), preferred_element_type=F32)


def logits_kernel(half, scalars, own_s, own_t, *refs):
    blocks = refs[:14]
    weight_s, weight_t, ids, out_s, out_t, stats, out_hidden = refs[14:21]
    hidden_s, hidden_t, here_s, here_t, logits_s, logits_t, spread, place_sems, sems = refs[21:]
    rows = out_s.shape[0] // 2
    width_s, width_t = hidden_s.shape[1], hidden_t.shape[1]
    parts = [slice(i * rows, (i + 1) * rows) for i in range(2)]
    heads = [
        (own_s, pl.ds(0, width_s), weight_s, out_s, hidden_s, here_s, logits_s),
        (own_t, pl.ds(width_s, width_t), weight_t, out_t, hidden_t, here_t, logits_t),
    ]
    placing, loads, stores = [], [], []
    for h, (own, columns, weight, out, hidden, here, logits) in enumerate(heads):
        placing.append(place(scalars, own, blocks, columns, hidden, half, place_sems.at[h]))
        loads.append(
            start_all([pltpu.make_async_copy(weight.at[at], here.at[at], sems.at[h, i]) for i, at in enumerate(parts)])
        )
        stores.append([pltpu.make_async_copy(logits.at[at], out.at[at], sems.at[h, 2 + i]) for i, at in enumerate(parts)])

    def product(h):
        _, _, _, _, hidden, here, logits = heads[h]
        wait_all(placing[h])
        for i, at in enumerate(parts):
            loads[h][i].wait()
            rows_product(here, hidden, logits, at)
            stores[h][i].start()

    tiles = [slice(j * 128, (j + 1) * 128) for j in range(out_s.shape[1] // 128)]

    def put(j, row, value):
        side, k = divmod(j, 2)
        spread[:, side, pl.ds(row * 2 + k, 1), :] = jnp.broadcast_to(value[None], (spread.shape[0], 1, 128))

    product(0)
    keep = pltpu.make_async_copy(hidden_s, out_hidden, sems.at[1, 4])
    keep.start()
    entry = lax.broadcasted_iota(I32, (out_s.shape[0], 128), 0) + scalars[15]
    for j, at in enumerate(tiles):
        s = logits_s[:, at]
        top = jnp.max(s, axis=0, keepdims=True)
        put(j, 0, top + jnp.log(jnp.sum(jnp.exp(s - top), axis=0, keepdims=True)))
        put(j, 3, jnp.sum(jnp.where(ids[:, at] == entry, s, 0.0), axis=0, keepdims=True))
    product(1)
    for j, at in enumerate(tiles):
        t = logits_t[:, at]
        top = jnp.max(t, axis=0, keepdims=True)
        exp_t = jnp.exp(t - top)
        total = jnp.sum(exp_t, axis=0, keepdims=True)
        put(j, 1, top + jnp.log(total))
        put(j, 2, jnp.sum(exp_t * (t - logits_s[:, at]), axis=0, keepdims=True) / total)
    last = pltpu.make_async_copy(spread, stats, sems.at[0, 4])
    last.start()
    wait_all(stores[0])
    wait_all(stores[1])
    last.wait()
    keep.wait()


def combine_kernel(every, out):
    stats = every[...]
    lse = stats[:, 0:4]
    top = jnp.max(lse, axis=0)
    total = top + jnp.log(jnp.sum(jnp.exp(lse - top[None]), axis=0))
    total_s, total_t = total[0:2], total[2:4]
    cross = jnp.sum(jnp.exp(stats[:, 2:4] - total_t[None]) * stats[:, 4:6], axis=0)
    picked = jnp.sum(stats[:, 6:8], axis=0)
    out[0:4] = total
    out[4:6] = cross - total_t + total_s
    out[6:8] = picked - total_s


def share_kernel(
    scalars, mine, other, factor, s_mine, t_mine, s_theirs, t_theirs, weight_mine, weight_theirs, share, out_t,
    small, totals, s_here, t_here, grad, grad_t, weight, part, sems,
):
    rows, width = weight_theirs.shape
    tokens = s_mine.shape[1]
    tile = weight.shape[2]
    steps = width // tile
    count = rows // 128
    figures = start_all(
        [pltpu.make_async_copy(mine, small.at[0], sems.at[4, 2]), pltpu.make_async_copy(other, small.at[1], sems.at[4, 3])]
    )
    logits = []
    for side, (s, t) in enumerate(((s_mine, t_mine), (s_theirs, t_theirs))):
        for j in range(count):
            at, to = pl.ds(j * 128, 128), pl.ds(side * rows + j * 128, 128)
            logits.append(
                start_all(
                    [
                        pltpu.make_async_copy(s.at[at], s_here.at[to], sems.at[side, j]),
                        pltpu.make_async_copy(t.at[at], t_here.at[to], sems.at[2 + side, j]),
                    ]
                )
            )
    waiting = []
    for k in range(steps):
        columns = pl.ds(pl.multiple_of(scalars[0] * width + k * tile, 128), tile)
        waiting.append(
            start_all(
                [
                    pltpu.make_async_copy(weight_mine.at[:, columns], weight.at[k, pl.ds(0, rows)], sems.at[5, k]),
                    pltpu.make_async_copy(
                        weight_theirs.at[:, pl.ds(k * tile, tile)], weight.at[k, pl.ds(rows, rows)], sems.at[6, k]
                    ),
                ]
            )
        )
    first = scalars[0] == 0
    wait_all(figures)
    low, high = jnp.where(first, small[0], small[1]), jnp.where(first, small[1], small[0])
    for j in range(tokens // 128):
        half, k = (low, high)[j // 2], j % 2
        for i in range(2):
            totals[i : i + 1, j * 128 : (j + 1) * 128] = half[2 * i + k : 2 * i + k + 1]
    stores = []
    for i, pair in enumerate(logits):
        wait_all(pair)
        at = slice(i * 128, (i + 1) * 128)
        value = factor[...] * (jnp.exp(s_here[at] - totals[0:1]) - jnp.exp(t_here[at] - totals[1:2]))
        if i < count:
            grad_t[at] = value.astype(BF16)
            stores.append(pltpu.make_async_copy(grad_t.at[pl.ds(i * 128, 128)], out_t.at[pl.ds(i * 128, 128)], sems.at[7, i]))
            stores[-1].start()
        grad[:, at] = value.T.astype(BF16)
    written = 0
    for k in range(steps):
        wait_all(waiting[k])
        product = jnp.dot(grad[...], weight[k], preferred_element_type=F32).astype(BF16)
        for j in range(tile // 256):
            high_at, low_at = divmod(k * tile + j * 256, share.shape[3])
            part[:, high_at, :, pl.ds(low_at, 256)] = product[:, j * 256 : (j + 1) * 256].reshape(share.shape[0], 16, 256)
        while (k + 1) * tile >= (written + 1) * share.shape[3]:
            stores.append(pltpu.make_async_copy(part.at[:, written], share.at[:, written], sems.at[4, written]))
            stores[-1].start()
            written += 1
    wait_all(stores)


def grad_weight_kernel(grad, hidden, out):
    out[...] = jnp.dot(grad[...], hidden[...], preferred_element_type=F32).astype(BF16)


def sum_kernel(parts, out):
    count = parts.shape[0] // 16
    total = jnp.sum(parts[0:count].astype(F32), axis=0)
    for i in range(1, 16):
        total += jnp.sum(parts[count * i : count * (i + 1)].astype(F32), axis=0)
    out[...] = jnp.broadcast_to(total.astype(BF16)[None], out.shape)


def assemble_kernel(scalars, mine, theirs, out):
    width = mine.shape[2]
    first = scalars[0] == 0
    low = jnp.where(first, mine[...], theirs[...])
    high = jnp.where(first, theirs[...], mine[...])
    for core, pieces in enumerate((low, high)):
        for v in range(8):
            column = (core * 2 + v % 2) * width
            out[v // 2 * 16 : v // 2 * 16 + 16, column : column + width] = pieces[v]


IN_VMEM = pl.BlockSpec(memory_space=pltpu.VMEM)
IN_HBM = pl.BlockSpec(memory_space=pltpu.HBM)
IN_SMEM = pl.BlockSpec(memory_space=pltpu.SMEM)


def params(limit=VMEM_BYTES):
    return pltpu.CompilerParams(vmem_limit_bytes=limit)


def shards(
    student_hidden,
    student_weight,
    teacher_hidden,
    teacher_weight,
    token_ids,
    group_ids,
    response_mask,
):
    own_rows = student_hidden.shape[0]
    half = own_rows // 2
    head_rows, width = student_weight.shape
    width_t = teacher_weight.shape[1]
    tokens = token_ids.shape[0]
    dp, vocab = lax.axis_index("dp"), lax.axis_index("vocab")
    core = vocab % 2
    odd = (vocab // 4) % 2
    half_width = width // 2
    scalars = jnp.stack(first_rows(core, odd, dp // 4, dp % 4, half) + [(dp * 16 + vocab) * head_rows]).astype(I32)
    core_scalar = core.astype(I32).reshape(1)

    kept = pl.pallas_call(
        half_kernel,
        in_specs=[IN_SMEM] + [IN_HBM] * 2,
        out_specs=IN_HBM,
        out_shape=jax.ShapeDtypeStruct((half, width + width_t), BF16),
        scratch_shapes=[pltpu.VMEM((half, width + width_t), BF16), pltpu.SemaphoreType.DMA((3,))],
        compiler_params=params(),
    )((core + odd - 2 * core * odd).astype(I32).reshape(1), student_hidden, teacher_hidden)
    blocks, weight_theirs = gather_tokens(
        kept, lax.dynamic_slice_in_dim(student_weight, (1 - core) * half_width, half_width, 1)
    )

    same_group = group_ids[:, None] == group_ids[None, :]
    lengths = jnp.sum(same_group.astype(F32), axis=1)
    token_weight = (response_mask.astype(F32) * SPAN / lengths).reshape(1, tokens)

    student_logits, teacher_logits, stats, hidden = pl.pallas_call(
        functools.partial(logits_kernel, half),
        in_specs=[IN_SMEM] + [IN_HBM] * 18 + [IN_VMEM],
        out_specs=[IN_HBM] * 4,
        out_shape=[
            jax.ShapeDtypeStruct((head_rows, tokens), F32),
            jax.ShapeDtypeStruct((head_rows, tokens), F32),
            jax.ShapeDtypeStruct((64, 2, 8, 128), F32),
            jax.ShapeDtypeStruct((tokens, width), BF16),
        ],
        scratch_shapes=[
            pltpu.VMEM((tokens, width), BF16),
            pltpu.VMEM((tokens, width_t), BF16),
            pltpu.VMEM((head_rows, width), BF16),
            pltpu.VMEM((head_rows, width_t), BF16),
            pltpu.VMEM((head_rows, tokens), F32),
            pltpu.VMEM((head_rows, tokens), F32),
            pltpu.VMEM((64, 2, 8, 128), F32),
            pltpu.SemaphoreType.DMA((2, 15)),
            pltpu.SemaphoreType.DMA((2, 5)),
        ],
        compiler_params=params(),
        cost_estimate=pl.CostEstimate(
            flops=2 * head_rows * tokens * (width + width_t), bytes_accessed=24_000_000, transcendentals=2 * head_rows * tokens
        ),
    )(scalars, student_hidden, teacher_hidden, *blocks, student_weight, teacher_weight, token_ids.reshape(1, tokens))

    stats, (student_logits, teacher_logits) = lax.optimization_barrier((stats, (student_logits, teacher_logits)))
    student_theirs, teacher_theirs = swap([student_logits, teacher_logits])
    every = lax.all_to_all(stats.reshape(128, 8, 128), BOTH, split_axis=0, concat_axis=0, tiled=True)
    mine = pl.pallas_call(
        combine_kernel,
        in_specs=[IN_VMEM],
        out_specs=IN_VMEM,
        out_shape=jax.ShapeDtypeStruct((8, 128), F32),
        compiler_params=params(4 * 1024 * 1024),
    )(every)
    other = send(mine, OTHER_CORE)

    groups, quarter = tokens // 16, half_width // 2
    share, grad_t = pl.pallas_call(
        share_kernel,
        in_specs=[IN_SMEM] + [IN_HBM] * 2 + [IN_VMEM] + [IN_HBM] * 6,
        out_specs=[IN_HBM, IN_HBM],
        out_shape=[
            jax.ShapeDtypeStruct((groups, 2, 16, quarter), BF16),
            jax.ShapeDtypeStruct((head_rows, tokens), BF16),
        ],
        scratch_shapes=[
            pltpu.VMEM((2, 8, 128), F32),
            pltpu.VMEM((8, tokens), F32),
            pltpu.VMEM((2 * head_rows, tokens), F32),
            pltpu.VMEM((2 * head_rows, tokens), F32),
            pltpu.VMEM((tokens, 2 * head_rows), BF16),
            pltpu.VMEM((head_rows, tokens), BF16),
            pltpu.VMEM((half_width // 512, 2 * head_rows, 512), BF16),
            pltpu.VMEM((groups, 2, 16, quarter), BF16),
            pltpu.SemaphoreType.DMA((8, 5)),
        ],
        compiler_params=params(),
        cost_estimate=pl.CostEstimate(flops=2 * head_rows * tokens * width, bytes_accessed=16_000_000, transcendentals=0),
    )(
        core_scalar, mine, other, token_weight, student_logits, teacher_logits, student_theirs, teacher_theirs,
        student_weight, weight_theirs,
    )
    parts = lax.all_to_all(
        share.reshape(64, 16, quarter), BOTH, split_axis=0, concat_axis=0, tiled=True, axis_index_groups=SAME_CORE
    )

    grad_weight = pl.pallas_call(
        grad_weight_kernel,
        grid=(width // 1024,),
        in_specs=[
            pl.BlockSpec((head_rows, tokens), lambda k: (0, 0)),
            pl.BlockSpec((tokens, 1024), lambda k: (0, k)),
        ],
        out_specs=pl.BlockSpec((head_rows, 1024), lambda k: (0, k)),
        out_shape=jax.ShapeDtypeStruct((head_rows, width), BF16),
        compiler_params=params(16 * 1024 * 1024),
        cost_estimate=pl.CostEstimate(flops=2 * head_rows * tokens * width, bytes_accessed=13_000_000, transcendentals=0),
    )(grad_t, hidden)
    low, high = jnp.where(core == 0, mine, other), jnp.where(core == 0, other, mine)
    kl_all = jnp.concatenate([low[4:6], high[4:6]]).reshape(tokens)
    logp_all = jnp.concatenate([low[6:8], high[6:8]]).reshape(tokens)
    kl_tok = lax.dynamic_slice_in_dim(kl_all, dp * own_rows, own_rows, 0)
    logp_tok = lax.dynamic_slice_in_dim(logp_all, dp * own_rows, own_rows, 0)
    parts, grad_weight, kl_tok, logp_tok = lax.optimization_barrier((parts, grad_weight, kl_tok, logp_tok))

    summed = pl.pallas_call(
        sum_kernel,
        in_specs=[IN_VMEM],
        out_specs=IN_VMEM,
        out_shape=jax.ShapeDtypeStruct((8, 16, quarter), BF16),
        compiler_params=params(8 * 1024 * 1024),
    )(parts)
    pieces_mine = lax.all_to_all(
        summed,
        BOTH, split_axis=0, concat_axis=0, tiled=True, axis_index_groups=SAME_TOKENS,
    )
    pieces_theirs = send(pieces_mine, OTHER_CORE)
    grad_hidden = pl.pallas_call(
        assemble_kernel,
        in_specs=[IN_SMEM] + [IN_VMEM] * 2,
        out_specs=IN_VMEM,
        out_shape=jax.ShapeDtypeStruct((own_rows, width), BF16),
        compiler_params=params(8 * 1024 * 1024),
    )(core_scalar, pieces_mine, pieces_theirs)
    return (kl_tok, logp_tok, grad_hidden, grad_weight)


def solution(mesh):
    in_specs = (
        P("dp", None),
        P(("dp", "vocab"), None),
        P("dp", None),
        P(("dp", "vocab"), None),
        P(),
        P(),
        P(),
    )
    out_specs = (P("dp"), P("dp"), P("dp", None), P(("dp", "vocab"), None))
    return jax.shard_map(shards, mesh=mesh, in_specs=in_specs, out_specs=out_specs, check_vma=False)
```

time: 436 us -> 151 us (0.35)
  blocking collectives: 269 us -> 13 us
  waiting for transfers between devices: 113 us -> 58.7 us
  starting transfers between devices: 0.08 us -> 34.5 us
  matrix products: 33.9 us -> 0 us
  Pallas kernels: 0 us -> 33.1 us
  between operations: 14.1 us -> 0.91 us
  local copies, waits for them, and re-layouts: 3.07 us -> 9.63 us
    psum x2 -> x0, blocking collectives: 178 us -> none  [shards(): lax.psum((local_s, jnp.sum(exp_t, axis=1), jnp.sum(exp_t * spread, axis=1...]
    all_gather x2 -> x0, waiting for transfers between devices: 111 us -> none  [the longest x1 56 us: shards(): hidden_all = lax.all_gather(student_hidden, 'dp', axis=0, tiled=True)]
    pmax x1 -> x0, blocking collectives: 64.3 us -> none  [shards(): lax.pmax((jnp.max(student_logits, axis=1), jnp.max(teacher_logits, axis=1...]
    all_to_all x0 -> x2, waiting for transfers between devices: none -> 37.7 us  [the longest x1 24.1 us: shards(): lax.all_to_all(share.reshape(64, 16, quarter), BOTH, split_axis=0, concat...]
    dot_general x4 -> x0, matrix products: 33.9 us -> none  [the longest x1 9.73 us: shards(): jnp.dot(grad_logits, student_weight, preferred_element_type=jnp.float32)]
    pallas_call x0 -> x7, Pallas kernels: none -> 33.1 us  [the longest x1 14.2 us: shards(): pl.pallas_call(functools.partial(logits_kernel, half), in_specs=[IN_SMEM]...]
    all_gather x1 -> x0, blocking collectives: 26.6 us -> none  [shards(): lax.all_gather(share.astype(jnp.bfloat16), 'vocab', axis=0, tiled=True)]
    ppermute x0 -> x19, starting transfers between devices: none -> 25.7 us  [send(): return lax.ppermute(value, BOTH, where)]
  transfers between devices with their start and end apart: 2 -> 21, of which waited for: 2 -> 14; matrix products, arithmetic and copies ran while one was open for 2% -> 4% of each run, Pallas kernels for 0% -> 14%
where the time goes in v1:
time: 151 us
  waiting for transfers between devices  58.7 us (39%)
  starting transfers between devices  34.5 us (23%)
  Pallas kernels  33.1 us (22%)
  blocking collectives  13 us (9%)
  local copies, waits for them, and re-layouts  9.63 us (6%)
    ppermute x19, starting transfers between devices, send(): return lax.ppermute(value, BOTH, where)  25.7 us
    all_to_all x1, waiting for transfers between devices, shards(): lax.all_to_all(share.reshape(64, 16, quarter), BOTH, split_axis=0, concat...  24.1 us
    ppermute x19, waiting for transfers between devices, send(): return lax.ppermute(value, BOTH, where)  21 us
    pallas_call x1, Pallas kernels, shards(): pl.pallas_call(functools.partial(logits_kernel, half), in_specs=[IN_SMEM]...  14.2 us
    all_to_all x1, waiting for transfers between devices, shards(): lax.all_to_all(stats.reshape(128, 8, 128), BOTH, split_axis=0, concat_axi...  13.6 us
    all_to_all x1, blocking collectives, shards(): lax.all_to_all(summed, BOTH, split_axis=0, concat_axis=0, tiled=True, axi...  13 us
    pallas_call x1, Pallas kernels, shards(): pl.pallas_call(share_kernel, in_specs=[IN_SMEM] + [IN_HBM] * 2 + [IN_VMEM...  9.47 us
    pallas_call x1, Pallas kernels, shards(): pl.pallas_call(grad_weight_kernel, grid=(width // 1024,), in_specs=[pl.Bl...  5.94 us
  transfers between devices with their start and end apart: 21, of which 14 were waited for; matrix products, arithmetic and copies ran while one was open for 4% of the time, Pallas kernels for 14%

profile of v1, /device:TPU:1, one launch (start us, length us, event | category | flops | bytes accessed | tf_op | source)
XLA Modules:
  0.0 150.7 jit_solution(3413933292692980776)
XLA Ops:
  0.7 1.9 %shard_map.102 = bf16[32,9216]{1,0:T(8,128)(2,1)} custom-call(s32[1]{0:T(128)} %bitcast.17.scalars, bf16[64,5120]{1,0:T(8,128)(2,1)} %own_s.1, bf16[64,4096]{1,0:T(8,128)(2,1)} %own_t.1), custom_call_target="tpu_custom_call" | custom-call | tf_op jit(solution)/shard_map/pallas_call | solution.py:320
  2.6 4.7 %collective-permute-start = (bf16[32,9216]{1,0:T(8,128)(2,1)}, bf16[32,9216]{1,0:T(8,128)(2,1)S(1)}, u32[]{:S(2)}, u32[]{:S(2)}) collective-permute-start(bf16[32,9216]{1,0:T(8,128)(2,1)} %shard_map.102), channel_id=1, source_target_pairs={{0,16},{1,49},{2,18},{3,51},{4,20},{5,53},{6,22},{7,55},{8,24},{9,... | collective-permute-start | bytes 1769480 | tf_op jit(solution)/shard_map/ppermute | solution.py:48
  7.2 2.5 %collective-permute-start.1 = (bf16[32,9216]{1,0:T(8,128)(2,1)}, bf16[32,9216]{1,0:T(8,128)(2,1)S(1)}, u32[]{:S(2)}, u32[]{:S(2)}) collective-permute-start(bf16[32,9216]{1,0:T(8,128)(2,1)} %shard_map.102), channel_id=1, source_target_pairs={{0,64},{1,67},{2,66},{3,65},{4,68},{5,71},{6,70},{7,69},{8,72},{9,... | collective-permute-start | bytes 1769480 | tf_op jit(solution)/shard_map/ppermute | solution.py:48
  9.7 3.8 %constant_dynamic-slice_fusion = bf16[640,2560]{1,0:T(8,128)(2,1)} fusion(bf16[640,5120]{1,0:T(8,128)(2,1)} %weight_mine.1, s32[]{:T(128)S(6)} %select_n.88), kind=kLoop, calls=%fused_computation.6 | loop fusion | bytes 6553604 | tf_op jit(solution)/shard_map/dynamic_slice | solution.py:329
  14.4 2.5 %collective-permute-done.1.refs_2_ = bf16[32,9216]{1,0:T(8,128)(2,1)S(1)} collective-permute-done((bf16[32,9216]{1,0:T(8,128)(2,1)}, bf16[32,9216]{1,0:T(8,128)(2,1)S(1)}, u32[]{:S(2)}, u32[]{:S(2)}) %collective-permute-start.1) | collective-permute-done | bytes 589856 | tf_op jit(solution)/shard_map/ppermute | solution.py:48
  16.9 3.0 %collective-permute-start.2 = (bf16[32,9216]{1,0:T(8,128)(2,1)S(1)}, bf16[32,9216]{1,0:T(8,128)(2,1)S(1)}, u32[]{:S(2)}, u32[]{:S(2)}) collective-permute-start(bf16[32,9216]{1,0:T(8,128)(2,1)S(1)} %collective-permute-done.refs_0_), channel_id=1, source_target_pairs={{0,64},{1,67},{2,66},{3,65},{4,68},{5,71},{6,70},{7,69},{8,72},{9,... | collective-permute-start | bytes 1769480 | tf_op jit(solution)/shard_map/ppermute | solution.py:48
  20.0 2.7 %collective-permute-start.4 = (bf16[32,9216]{1,0:T(8,128)(2,1)S(1)}, bf16[32,9216]{1,0:T(8,128)(2,1)S(1)}, u32[]{:S(2)}, u32[]{:S(2)}) collective-permute-start(bf16[32,9216]{1,0:T(8,128)(2,1)S(1)} %collective-permute-done.refs_0_), channel_id=1, source_target_pairs={{0,4},{1,13},{2,6},{3,15},{4,8},{5,1},{6,10},{7,3},{8,12},{9,5},{1... | collective-permute-start | bytes 1769480 | tf_op jit(solution)/shard_map/ppermute | solution.py:48
  23.2 3.5 %collective-permute-done.2.refs_4_ = bf16[32,9216]{1,0:T(8,128)(2,1)S(1)} collective-permute-done((bf16[32,9216]{1,0:T(8,128)(2,1)S(1)}, bf16[32,9216]{1,0:T(8,128)(2,1)S(1)}, u32[]{:S(2)}, u32[]{:S(2)}) %collective-permute-start.2) | collective-permute-done | bytes 589856 | tf_op jit(solution)/shard_map/ppermute | solution.py:48
  26.7 2.2 %collective-permute-done.3.refs_3_ = bf16[32,9216]{1,0:T(8,128)(2,1)S(1)} collective-permute-done((bf16[32,9216]{1,0:T(8,128)(2,1)S(1)}, bf16[32,9216]{1,0:T(8,128)(2,1)S(1)}, u32[]{:S(2)}, u32[]{:S(2)}) %collective-permute-start.3) | collective-permute-done | bytes 589856 | tf_op jit(solution)/shard_map/ppermute | solution.py:48
  30.8 2.7 %collective-permute-start.7 = (bf16[32,9216]{1,0:T(8,128)(2,1)S(1)}, bf16[32,9216]{1,0:T(8,128)(2,1)S(1)}, u32[]{:S(2)}, u32[]{:S(2)}) collective-permute-start(bf16[32,9216]{1,0:T(8,128)(2,1)S(1)} %collective-permute-done.3.refs_3_), channel_id=1, source_target_pairs={{0,64},{1,67},{2,66},{3,65},{4,68},{5,71},{6,70},{7,69},{8,72},{9,... | collective-permute-start | bytes 1769480 | tf_op jit(solution)/shard_map/ppermute | solution.py:48
  35.5 4.8 %collective-permute-done.7.refs_6_ = bf16[32,9216]{1,0:T(8,128)(2,1)S(1)} collective-permute-done((bf16[32,9216]{1,0:T(8,128)(2,1)S(1)}, bf16[32,9216]{1,0:T(8,128)(2,1)S(1)}, u32[]{:S(2)}, u32[]{:S(2)}) %collective-permute-start.7) | collective-permute-done | bytes 589856 | tf_op jit(solution)/shard_map/ppermute | solution.py:48
  40.3 2.2 %collective-permute-done.8.refs_5_ = bf16[32,9216]{1,0:T(8,128)(2,1)S(1)} collective-permute-done((bf16[32,9216]{1,0:T(8,128)(2,1)S(1)}, bf16[32,9216]{1,0:T(8,128)(2,1)S(1)}, u32[]{:S(2)}, u32[]{:S(2)}) %collective-permute-start.8) | collective-permute-done | bytes 589856 | tf_op jit(solution)/shard_map/ppermute | solution.py:48
  42.5 2.7 %collective-permute-start.12 = (bf16[32,9216]{1,0:T(8,128)(2,1)S(1)}, bf16[32,9216]{1,0:T(8,128)(2,1)S(1)}, u32[]{:S(2)}, u32[]{:S(2)}) collective-permute-start(bf16[32,9216]{1,0:T(8,128)(2,1)S(1)} %collective-permute-done.8.refs_5_), channel_id=1, source_target_pairs={{0,1},{1,0},{2,3},{3,2},{4,5},{5,4},{6,7},{7,6},{8,9},{9,8},{10,11... | collective-permute-start | bytes 1769480 | tf_op jit(solution)/shard_map/ppermute | solution.py:48
  45.3 1.5 %collective-permute-done.12.refs_12_ = bf16[32,9216]{1,0:T(8,128)(2,1)S(1)} collective-permute-done((bf16[32,9216]{1,0:T(8,128)(2,1)S(1)}, bf16[32,9216]{1,0:T(8,128)(2,1)S(1)}, u32[]{:S(2)}, u32[]{:S(2)}) %collective-permute-start.12) | collective-permute-done | bytes 589856 | tf_op jit(solution)/shard_map/ppermute | solution.py:48
  49.6 14.2 %shard_map.103 = (f32[640,512]{1,0:T(8,128)}, f32[640,512]{1,0:T(8,128)}, f32[64,2,8,128]{3,2,1,0:T(8,128)}, bf16[512,5120]{1,0:T(8,128)(2,1)}) custom-call(s32[16]{0:T(128)} %stack.67.scalars, bf16[64,5120]{1,0:T(8,128)(2,1)} %own_s.1, bf16[64,4096]{1,0:T(8,128)(2,1)} %own_t.1, bf16[32,9216]{1,0:T(8,128)(2,1)} %copy-done.8, bf16[32,9216]{1,0:T(8,128)(2,1)} %copy-done.12, ...), custom_call_target="tpu_custom_call" | custom-call | flops 6039797760 | bytes 24000000 | tf_op jit(solution)/shard_map/pallas_call | solution.py:336
  64.6 4.0 %all-to-all-start = ((f32[128,8,128]{2,1,0:T(8,128)}), f32[128,8,128]{2,1,0:T(8,128)S(1)}, u32[]{:S(2)}, u32[]{:S(2)}) async-start(f32[128,8,128]{2,1,0:T(8,128)} %bitcast.27), calls=%async_computation | async-start | bytes 1048576 | tf_op jit(solution)/shard_map/all_to_all | solution.py:365
  68.8 13.6 %all-to-all-done.every = f32[128,8,128]{2,1,0:T(8,128)S(1)} async-done(((f32[128,8,128]{2,1,0:T(8,128)}), f32[128,8,128]{2,1,0:T(8,128)S(1)}, u32[]{:S(2)}, u32[]{:S(2)}) %all-to-all-start) | async-done | bytes 524320 | tf_op jit(solution)/shard_map/all_to_all | solution.py:365
  84.6 9.5 %shard_map.105 = (bf16[32,2,16,1280]{3,2,1,0:T(8,128)(2,1)}, bf16[640,512]{1,0:T(8,128)(2,1)}) custom-call(s32[1]{0:T(128)} %bitcast.scalars, f32[8,128]{1,0:T(8,128)} %copy-done.2, f32[8,128]{1,0:T(8,128)} %copy-done.4, f32[1,512]{1,0:T(1,128)} %bitcast.28, f32[640,512]{1,0:T(8,128)} %get-tuple-element.52.s_mine, f32[640,512]{1,0:T(8,128)} %get-tuple-element.53.t_mine, ...), custom_call_target="tpu_custom_call" | custom-call | flops 3355443200 | bytes 16000000 | tf_op jit(solution)/shard_map/pallas_call | solution.py:376
  94.2 4.9 %all-to-all-start.1 = ((bf16[64,16,1280]{2,1,0:T(8,128)(2,1)}), bf16[64,16,1280]{2,1,0:T(8,128)(2,1)S(1)}, u32[]{:S(2)}, u32[]{:S(2)}) async-start(bf16[64,16,1280]{2,1,0:T(8,128)(2,1)} %bitcast.26), calls=%async_computation.1 | async-start | bytes 5242880 | tf_op jit(solution)/shard_map/all_to_all | solution.py:401
  100.3 2.5 %copy-done = bf16[512,5120]{1,0:T(8,128)(2,1)S(1)} copy-done((bf16[512,5120]{1,0:T(8,128)(2,1)S(1)}, bf16[512,5120]{1,0:T(8,128)(2,1)}, u32[]{:S(2)}) %copy-start) | copy-done | bytes 5242904
  102.8 5.9 %shard_map.106 = bf16[640,5120]{1,0:T(8,128)(2,1)} custom-call(bf16[640,512]{1,0:T(8,128)(2,1)S(1)} %copy-done.1, bf16[512,5120]{1,0:T(8,128)(2,1)S(1)} %copy-done), custom_call_target="tpu_custom_call" | custom-call | flops 3355443200 | bytes 13000000 | tf_op jit(solution)/shard_map/pallas_call | solution.py:405
  108.7 24.1 %all-to-all-done.1.parts = bf16[64,16,1280]{2,1,0:T(8,128)(2,1)S(1)} async-done(((bf16[64,16,1280]{2,1,0:T(8,128)(2,1)}), bf16[64,16,1280]{2,1,0:T(8,128)(2,1)S(1)}, u32[]{:S(2)}, u32[]{:S(2)}) %all-to-all-start.1) | async-done | bytes 2621472 | tf_op jit(solution)/shard_map/all_to_all | solution.py:401
  133.2 13.0 %all_to_all.15.mine = bf16[8,16,1280]{2,1,0:T(8,128)(2,1)S(1)} all-to-all(bf16[8,16,1280]{2,1,0:T(8,128)(2,1)S(1)} %shard_map.107), channel_id=1, replica_groups={{0,2,4,6,8,10,12,14},{1,3,5,7,9,11,13,15},{16,18,20,22,24,26,28,30},{17..., dimensions={0} | all-to-all | bytes 655360 | tf_op jit(solution)/shard_map/all_to_all | solution.py:431
  146.2 2.4 %collective-permute-start.18 = (bf16[8,16,1280]{2,1,0:T(8,128)(2,1)S(1)}, bf16[8,16,1280]{2,1,0:T(8,128)(2,1)S(1)}, u32[]{:S(2)}, u32[]{:S(2)}) collective-permute-start(bf16[8,16,1280]{2,1,0:T(8,128)(2,1)S(1)} %all_to_all.15.mine), channel_id=1, source_target_pairs={{0,1},{1,0},{2,3},{3,2},{4,5},{5,4},{6,7},{7,6},{8,9},{9,8},{10,11... | collective-permute-start | bytes 983048 | tf_op jit(solution)/shard_map/ppermute | solution.py:48
  (80 shorter events, 15.2 us)
Async XLA Ops:
  2.6 11.8 %collective-permute-start = (bf16[32,9216]{1,0:T(8,128)(2,1)}, bf16[32,9216]{1,0:T(8,128)(2,1)S(1)}, u32[]{:S(2)}, u32[]{:S(2)}) collective-permute-start(bf16[32,9216]{1,0:T(8,128)(2,1)} %shard_map.102), channel_id=1, source_target_pairs={{0,16},{1,49},{2,18},{3,51},{4,20},{5,53},{6,22},{7,55},{8,24},{9,... | collective-permute-start | bytes 1769480 | tf_op jit(solution)/shard_map/ppermute | solution.py:48
  7.2 9.6 %collective-permute-start.1 = (bf16[32,9216]{1,0:T(8,128)(2,1)}, bf16[32,9216]{1,0:T(8,128)(2,1)S(1)}, u32[]{:S(2)}, u32[]{:S(2)}) collective-permute-start(bf16[32,9216]{1,0:T(8,128)(2,1)} %shard_map.102), channel_id=1, source_target_pairs={{0,64},{1,67},{2,66},{3,65},{4,68},{5,71},{6,70},{7,69},{8,72},{9,... | collective-permute-start | bytes 1769480 | tf_op jit(solution)/shard_map/ppermute | solution.py:48
  14.4 35.2 %copy-start.8 = (bf16[32,9216]{1,0:T(8,128)(2,1)}, bf16[32,9216]{1,0:T(8,128)(2,1)S(1)}, u32[]{:S(2)}) copy-start(bf16[32,9216]{1,0:T(8,128)(2,1)S(1)} %collective-permute-done.refs_0_) | copy-start | bytes 1769476
  16.9 32.7 %copy-start.9 = (bf16[32,9216]{1,0:T(8,128)(2,1)}, bf16[32,9216]{1,0:T(8,128)(2,1)S(1)}, u32[]{:S(2)}) copy-start(bf16[32,9216]{1,0:T(8,128)(2,1)S(1)} %collective-permute-done.1.refs_2_) | copy-start | bytes 1769476
  16.9 9.8 %collective-permute-start.2 = (bf16[32,9216]{1,0:T(8,128)(2,1)S(1)}, bf16[32,9216]{1,0:T(8,128)(2,1)S(1)}, u32[]{:S(2)}, u32[]{:S(2)}) collective-permute-start(bf16[32,9216]{1,0:T(8,128)(2,1)S(1)} %collective-permute-done.refs_0_), channel_id=1, source_target_pairs={{0,64},{1,67},{2,66},{3,65},{4,68},{5,71},{6,70},{7,69},{8,72},{9,... | collective-permute-start | bytes 1769480 | tf_op jit(solution)/shard_map/ppermute | solution.py:48
  19.9 9.0 %collective-permute-start.3 = (bf16[32,9216]{1,0:T(8,128)(2,1)S(1)}, bf16[32,9216]{1,0:T(8,128)(2,1)S(1)}, u32[]{:S(2)}, u32[]{:S(2)}) collective-permute-start(bf16[32,9216]{1,0:T(8,128)(2,1)S(1)} %collective-permute-done.refs_0_), channel_id=1, source_target_pairs={{0,16},{1,49},{2,18},{3,51},{4,20},{5,53},{6,22},{7,55},{8,24},{9,... | collective-permute-start | bytes 1769480 | tf_op jit(solution)/shard_map/ppermute | solution.py:48
  20.0 9.6 %collective-permute-start.4 = (bf16[32,9216]{1,0:T(8,128)(2,1)S(1)}, bf16[32,9216]{1,0:T(8,128)(2,1)S(1)}, u32[]{:S(2)}, u32[]{:S(2)}) collective-permute-start(bf16[32,9216]{1,0:T(8,128)(2,1)S(1)} %collective-permute-done.refs_0_), channel_id=1, source_target_pairs={{0,4},{1,13},{2,6},{3,15},{4,8},{5,1},{6,10},{7,3},{8,12},{9,5},{1... | collective-permute-start | bytes 1769480 | tf_op jit(solution)/shard_map/ppermute | solution.py:48
  22.7 6.8 %collective-permute-start.5 = (bf16[32,9216]{1,0:T(8,128)(2,1)S(1)}, bf16[32,9216]{1,0:T(8,128)(2,1)S(1)}, u32[]{:S(2)}, u32[]{:S(2)}) collective-permute-start(bf16[32,9216]{1,0:T(8,128)(2,1)S(1)} %collective-permute-done.refs_0_), channel_id=1, source_target_pairs={{0,1},{1,0},{2,3},{3,2},{4,5},{5,4},{6,7},{7,6},{8,9},{9,8},{10,11... | collective-permute-start | bytes 1769480 | tf_op jit(solution)/shard_map/ppermute | solution.py:48
  22.7 6.8 %collective-permute-start.6 = (bf16[32,9216]{1,0:T(8,128)(2,1)S(1)}, bf16[32,9216]{1,0:T(8,128)(2,1)S(1)}, u32[]{:S(2)}, u32[]{:S(2)}) collective-permute-start(bf16[32,9216]{1,0:T(8,128)(2,1)S(1)} %collective-permute-done.1.refs_2_), channel_id=1, source_target_pairs={{0,1},{1,0},{2,3},{3,2},{4,5},{5,4},{6,7},{7,6},{8,9},{9,8},{10,11... | collective-permute-start | bytes 1769480 | tf_op jit(solution)/shard_map/ppermute | solution.py:48
  29.6 5.4 %collective-permute-start.10 = (bf16[32,9216]{1,0:T(8,128)(2,1)S(1)}, bf16[32,9216]{1,0:T(8,128)(2,1)S(1)}, u32[]{:S(2)}, u32[]{:S(2)}) collective-permute-start(bf16[32,9216]{1,0:T(8,128)(2,1)S(1)} %collective-permute-done.3.refs_3_), channel_id=1, source_target_pairs={{0,1},{1,0},{2,3},{3,2},{4,5},{5,4},{6,7},{7,6},{8,9},{9,8},{10,11... | collective-permute-start | bytes 1769480 | tf_op jit(solution)/shard_map/ppermute | solution.py:48
  30.8 9.5 %collective-permute-start.7 = (bf16[32,9216]{1,0:T(8,128)(2,1)S(1)}, bf16[32,9216]{1,0:T(8,128)(2,1)S(1)}, u32[]{:S(2)}, u32[]{:S(2)}) collective-permute-start(bf16[32,9216]{1,0:T(8,128)(2,1)S(1)} %collective-permute-done.3.refs_3_), channel_id=1, source_target_pairs={{0,64},{1,67},{2,66},{3,65},{4,68},{5,71},{6,70},{7,69},{8,72},{9,... | collective-permute-start | bytes 1769480 | tf_op jit(solution)/shard_map/ppermute | solution.py:48
  33.4 2.0 %collective-permute-start.11 = (bf16[32,9216]{1,0:T(8,128)(2,1)S(1)}, bf16[32,9216]{1,0:T(8,128)(2,1)S(1)}, u32[]{:S(2)}, u32[]{:S(2)}) collective-permute-start(bf16[32,9216]{1,0:T(8,128)(2,1)S(1)} %collective-permute-done.4.refs_1_), channel_id=1, source_target_pairs={{0,1},{1,0},{2,3},{3,2},{4,5},{5,4},{6,7},{7,6},{8,9},{9,8},{10,11... | collective-permute-start | bytes 1769480 | tf_op jit(solution)/shard_map/ppermute | solution.py:48
  33.4 9.0 %collective-permute-start.8 = (bf16[32,9216]{1,0:T(8,128)(2,1)S(1)}, bf16[32,9216]{1,0:T(8,128)(2,1)S(1)}, u32[]{:S(2)}, u32[]{:S(2)}) collective-permute-start(bf16[32,9216]{1,0:T(8,128)(2,1)S(1)} %collective-permute-done.2.refs_4_), channel_id=1, source_target_pairs={{0,4},{1,13},{2,6},{3,15},{4,8},{5,1},{6,10},{7,3},{8,12},{9,5},{1... | collective-permute-start | bytes 1769480 | tf_op jit(solution)/shard_map/ppermute | solution.py:48
  35.0 7.5 %collective-permute-start.9 = (bf16[32,9216]{1,0:T(8,128)(2,1)S(1)}, bf16[32,9216]{1,0:T(8,128)(2,1)S(1)}, u32[]{:S(2)}, u32[]{:S(2)}) collective-permute-start(bf16[32,9216]{1,0:T(8,128)(2,1)S(1)} %collective-permute-done.2.refs_4_), channel_id=1, source_target_pairs={{0,1},{1,0},{2,3},{3,2},{4,5},{5,4},{6,7},{7,6},{8,9},{9,8},{10,11... | collective-permute-start | bytes 1769480 | tf_op jit(solution)/shard_map/ppermute | solution.py:48
  42.5 4.3 %collective-permute-start.12 = (bf16[32,9216]{1,0:T(8,128)(2,1)S(1)}, bf16[32,9216]{1,0:T(8,128)(2,1)S(1)}, u32[]{:S(2)}, u32[]{:S(2)}) collective-permute-start(bf16[32,9216]{1,0:T(8,128)(2,1)S(1)} %collective-permute-done.8.refs_5_), channel_id=1, source_target_pairs={{0,1},{1,0},{2,3},{3,2},{4,5},{5,4},{6,7},{7,6},{8,9},{9,8},{10,11... | collective-permute-start | bytes 1769480 | tf_op jit(solution)/shard_map/ppermute | solution.py:48
  45.2 2.5 %collective-permute-start.13 = (bf16[32,9216]{1,0:T(8,128)(2,1)S(1)}, bf16[32,9216]{1,0:T(8,128)(2,1)S(1)}, u32[]{:S(2)}, u32[]{:S(2)}) collective-permute-start(bf16[32,9216]{1,0:T(8,128)(2,1)S(1)} %collective-permute-done.7.refs_6_), channel_id=1, source_target_pairs={{0,1},{1,0},{2,3},{3,2},{4,5},{5,4},{6,7},{7,6},{8,9},{9,8},{10,11... | collective-permute-start | bytes 1769480 | tf_op jit(solution)/shard_map/ppermute | solution.py:48
  48.5 35.6 %collective-permute-start.17 = (bf16[640,2560]{1,0:T(8,128)(2,1)}, bf16[640,2560]{1,0:T(8,128)(2,1)}, u32[]{:S(2)}, u32[]{:S(2)}) collective-permute-start(bf16[640,2560]{1,0:T(8,128)(2,1)} %constant_dynamic-slice_fusion), channel_id=1, source_target_pairs={{0,1},{1,0},{2,3},{3,2},{4,5},{5,4},{6,7},{7,6},{8,9},{9,8},{10,11... | collective-permute-start | bytes 9830408 | tf_op jit(solution)/shard_map/ppermute | solution.py:48
  49.6 33.7 %copy-start.7 = (s32[512]{0:T(512)S(1)}, s32[512]{0:T(512)}, u32[]{:S(2)}) copy-start(s32[512]{0:T(512)} %param.13) | copy-start | bytes 6148
  63.8 20.3 %collective-permute-start.15 = (f32[640,512]{1,0:T(8,128)}, f32[640,512]{1,0:T(8,128)}, u32[]{:S(2)}, u32[]{:S(2)}) collective-permute-start(f32[640,512]{1,0:T(8,128)} %get-tuple-element.52.s_mine), channel_id=1, source_target_pairs={{0,1},{1,0},{2,3},{3,2},{4,5},{5,4},{6,7},{7,6},{8,9},{9,8},{10,11... | collective-permute-start | bytes 3932168 | tf_op jit(solution)/shard_map/ppermute | solution.py:48
  64.2 19.9 %collective-permute-start.16 = (f32[640,512]{1,0:T(8,128)}, f32[640,512]{1,0:T(8,128)}, u32[]{:S(2)}, u32[]{:S(2)}) collective-permute-start(f32[640,512]{1,0:T(8,128)} %get-tuple-element.53.t_mine), channel_id=1, source_target_pairs={{0,1},{1,0},{2,3},{3,2},{4,5},{5,4},{6,7},{7,6},{8,9},{9,8},{10,11... | collective-permute-start | bytes 3932168 | tf_op jit(solution)/shard_map/ppermute | solution.py:48
  64.6 17.8 %all-to-all-start = ((f32[128,8,128]{2,1,0:T(8,128)}), f32[128,8,128]{2,1,0:T(8,128)S(1)}, u32[]{:S(2)}, u32[]{:S(2)}) async-start(f32[128,8,128]{2,1,0:T(8,128)} %bitcast.27), calls=%async_computation | async-start | bytes 1048576 | tf_op jit(solution)/shard_map/all_to_all | solution.py:365
  82.8 1.3 collective-permute-start.14
  94.2 38.7 %all-to-all-start.1 = ((bf16[64,16,1280]{2,1,0:T(8,128)(2,1)}), bf16[64,16,1280]{2,1,0:T(8,128)(2,1)S(1)}, u32[]{:S(2)}, u32[]{:S(2)}) async-start(bf16[64,16,1280]{2,1,0:T(8,128)(2,1)} %bitcast.26), calls=%async_computation.1 | async-start | bytes 5242880 | tf_op jit(solution)/shard_map/all_to_all | solution.py:401
  146.2 3.7 %collective-permute-start.18 = (bf16[8,16,1280]{2,1,0:T(8,128)(2,1)S(1)}, bf16[8,16,1280]{2,1,0:T(8,128)(2,1)S(1)}, u32[]{:S(2)}, u32[]{:S(2)}) collective-permute-start(bf16[8,16,1280]{2,1,0:T(8,128)(2,1)S(1)} %all_to_all.15.mine), channel_id=1, source_target_pairs={{0,1},{1,0},{2,3},{3,2},{4,5},{5,4},{6,7},{7,6},{8,9},{9,8},{10,11... | collective-permute-start | bytes 983048 | tf_op jit(solution)/shard_map/ppermute | solution.py:48
  (19 other events, 172.3 us)

commit v2 on v1

--- a/solution.py
+++ b/solution.py
@@ -57,16 +57,18 @@
     return [send(block, OTHER_CORE) for block in blocks]
 
 
-def gather_tokens(kept, weight_columns):
-    near_z, near_x, weight_columns = lax.optimization_barrier((send(kept, ALONG_Z), send(kept, ALONG_X), weight_columns))
+def gather_tokens(kept, others):
+    near_z, near_x, others = lax.optimization_barrier((send(kept, ALONG_Z), send(kept, ALONG_X), others))
     second = [send(near_z, ALONG_X), send(near_z, ALONG_Z), send(near_z, ALONG_Y)] + swap([near_z, near_x])
     near_zx, far_z, rest_z, o_near_z, o_near_x = lax.optimization_barrier(second)
     third = [send(far_z, ALONG_X), send(near_zx, ALONG_Y)] + swap([near_zx, far_z, rest_z])
     far_zx, rest_zx, o_near_zx, o_far_z, o_rest_z = lax.optimization_barrier(third)
+    scalars, core_scalar, token_weight, ids, weight_columns = others
     o_rest_zx, o_far_zx, weight_columns = lax.optimization_barrier((*swap([rest_zx, far_zx]), weight_columns))
+    weight_theirs = send(weight_columns, OTHER_CORE)
     mine = [near_z, rest_z, near_x, far_z, near_zx, rest_zx, far_zx]
     theirs = [o_near_z, o_rest_z, o_near_x, o_far_z, o_near_zx, o_rest_zx, o_far_zx]
-    return mine + theirs, send(weight_columns, OTHER_CORE)
+    return mine + theirs, (scalars, core_scalar, token_weight, ids, weight_theirs)
 
 
 def first_rows(core, odd, x_lo, z, half):
@@ -128,7 +130,7 @@
 def logits_kernel(half, scalars, own_s, own_t, *refs):
     blocks = refs[:14]
     weight_s, weight_t, ids, out_s, out_t, stats, out_hidden = refs[14:21]
-    hidden_s, hidden_t, here_s, here_t, logits_s, logits_t, spread, place_sems, sems = refs[21:]
+    hidden_s, hidden_t, here_s, here_t, logits_s, logits_t, place_sems, sems = refs[21:]
     rows = out_s.shape[0] // 2
     width_s, width_t = hidden_s.shape[1], hidden_t.shape[1]
     parts = [slice(i * rows, (i + 1) * rows) for i in range(2)]
@@ -138,27 +140,34 @@
     ]
     placing, loads, stores = [], [], []
     for h, (own, columns, weight, out, hidden, here, logits) in enumerate(heads):
+        loads.append([pltpu.make_async_copy(weight.at[at], here.at[at], sems.at[h, i]) for i, at in enumerate(parts)])
+        stores.append([pltpu.make_async_copy(logits.at[at], out.at[at], sems.at[h, 2 + i]) for i, at in enumerate(parts)])
+
+    def start_placing(h):
+        own, columns, _, _, hidden, _, _ = heads[h]
         placing.append(place(scalars, own, blocks, columns, hidden, half, place_sems.at[h]))
-        loads.append(
-            start_all([pltpu.make_async_copy(weight.at[at], here.at[at], sems.at[h, i]) for i, at in enumerate(parts)])
-        )
-        stores.append([pltpu.make_async_copy(logits.at[at], out.at[at], sems.at[h, 2 + i]) for i, at in enumerate(parts)])
-
-    def product(h):
+
+    def product(h, i):
         _, _, _, _, hidden, here, logits = heads[h]
-        wait_all(placing[h])
-        for i, at in enumerate(parts):
-            loads[h][i].wait()
-            rows_product(here, hidden, logits, at)
-            stores[h][i].start()
+        rows_product(here, hidden, logits, parts[i])
+        stores[h][i].start()
 
     tiles = [slice(j * 128, (j + 1) * 128) for j in range(out_s.shape[1] // 128)]
 
     def put(j, row, value):
         side, k = divmod(j, 2)
-        spread[:, side, pl.ds(row * 2 + k, 1), :] = jnp.broadcast_to(value[None], (spread.shape[0], 1, 128))
-
-    product(0)
+        stats[:, side, pl.ds(row * 2 + k, 1), :] = jnp.broadcast_to(value[None], (stats.shape[0], 1, 128))
+
+    loads[0][0].start()
+    start_placing(0)
+    wait_all(placing[0])
+    loads[0][1].start()
+    loads[0][0].wait()
+    start_placing(1)
+    product(0, 0)
+    loads[0][1].wait()
+    start_all(loads[1])
+    product(0, 1)
     keep = pltpu.make_async_copy(hidden_s, out_hidden, sems.at[1, 4])
     keep.start()
     entry = lax.broadcasted_iota(I32, (out_s.shape[0], 128), 0) + scalars[15]
@@ -167,7 +176,10 @@
         top = jnp.max(s, axis=0, keepdims=True)
         put(j, 0, top + jnp.log(jnp.sum(jnp.exp(s - top), axis=0, keepdims=True)))
         put(j, 3, jnp.sum(jnp.where(ids[:, at] == entry, s, 0.0), axis=0, keepdims=True))
-    product(1)
+    wait_all(placing[1])
+    for i in range(2):
+        loads[1][i].wait()
+        product(1, i)
     for j, at in enumerate(tiles):
         t = logits_t[:, at]
         top = jnp.max(t, axis=0, keepdims=True)
@@ -175,11 +187,8 @@
         total = jnp.sum(exp_t, axis=0, keepdims=True)
         put(j, 1, top + jnp.log(total))
         put(j, 2, jnp.sum(exp_t * (t - logits_s[:, at]), axis=0, keepdims=True) / total)
-    last = pltpu.make_async_copy(spread, stats, sems.at[0, 4])
-    last.start()
     wait_all(stores[0])
     wait_all(stores[1])
-    last.wait()
     keep.wait()
 
 
@@ -196,12 +205,28 @@
     out[6:8] = picked - total_s
 
 
+def join_kernel(s_mine, t_mine, s_theirs, t_theirs, s_out, t_out, here, sems):
+    rows = s_mine.shape[0]
+    given = ((s_mine, t_mine), (s_theirs, t_theirs))
+    loads = [
+        pltpu.make_async_copy(given[side][h], here.at[h, pl.ds(side * rows, rows)], sems.at[2 * h + side])
+        for h in range(2)
+        for side in range(2)
+    ]
+    stores = [pltpu.make_async_copy(here.at[h], out, sems.at[4 + h]) for h, out in enumerate((s_out, t_out))]
+    start_all(loads)
+    for h in range(2):
+        wait_all(loads[2 * h : 2 * h + 2])
+        stores[h].start()
+    wait_all(stores)
+
+
 def share_kernel(
-    scalars, mine, other, factor, s_mine, t_mine, s_theirs, t_theirs, weight_mine, weight_theirs, share, out_t,
+    scalars, mine, other, factor, student, teacher, weight_mine, weight_theirs, share, out_t,
     small, totals, s_here, t_here, grad, grad_t, weight, part, sems,
 ):
     rows, width = weight_theirs.shape
-    tokens = s_mine.shape[1]
+    tokens = student.shape[1]
     tile = weight.shape[2]
     steps = width // tile
     count = rows // 128
@@ -209,19 +234,22 @@
         [pltpu.make_async_copy(mine, small.at[0], sems.at[4, 2]), pltpu.make_async_copy(other, small.at[1], sems.at[4, 3])]
     )
     logits = []
-    for side, (s, t) in enumerate(((s_mine, t_mine), (s_theirs, t_theirs))):
-        for j in range(count):
-            at, to = pl.ds(j * 128, 128), pl.ds(side * rows + j * 128, 128)
-            logits.append(
-                start_all(
-                    [
-                        pltpu.make_async_copy(s.at[at], s_here.at[to], sems.at[side, j]),
-                        pltpu.make_async_copy(t.at[at], t_here.at[to], sems.at[2 + side, j]),
-                    ]
-                )
+    for j in range(2 * count):
+        at = pl.ds(j * 128, 128)
+        logits.append(
+            start_all(
+                [
+                    pltpu.make_async_copy(student.at[at], s_here.at[at], sems.at[0, j]),
+                    pltpu.make_async_copy(teacher.at[at], t_here.at[at], sems.at[1, j]),
+                ]
             )
+        )
     waiting = []
-    for k in range(steps):
+
+    def load_weight():
+        k = len(waiting)
+        if k == steps:
+            return
         columns = pl.ds(pl.multiple_of(scalars[0] * width + k * tile, 128), tile)
         waiting.append(
             start_all(
@@ -233,6 +261,8 @@
                 ]
             )
         )
+
+    load_weight()
     first = scalars[0] == 0
     wait_all(figures)
     low, high = jnp.where(first, small[0], small[1]), jnp.where(first, small[1], small[0])
@@ -250,9 +280,12 @@
             stores.append(pltpu.make_async_copy(grad_t.at[pl.ds(i * 128, 128)], out_t.at[pl.ds(i * 128, 128)], sems.at[7, i]))
             stores[-1].start()
         grad[:, at] = value.T.astype(BF16)
+        if i in (count - 1, 2 * count - 3):
+            load_weight()
     written = 0
     for k in range(steps):
         wait_all(waiting[k])
+        load_weight()
         product = jnp.dot(grad[...], weight[k], preferred_element_type=F32).astype(BF16)
         for j in range(tile // 256):
             high_at, low_at = divmod(k * tile + j * 256, share.shape[3])
@@ -325,18 +358,18 @@
         scratch_shapes=[pltpu.VMEM((half, width + width_t), BF16), pltpu.SemaphoreType.DMA((3,))],
         compiler_params=params(),
     )((core + odd - 2 * core * odd).astype(I32).reshape(1), student_hidden, teacher_hidden)
-    blocks, weight_theirs = gather_tokens(
-        kept, lax.dynamic_slice_in_dim(student_weight, (1 - core) * half_width, half_width, 1)
-    )
-
     same_group = group_ids[:, None] == group_ids[None, :]
     lengths = jnp.sum(same_group.astype(F32), axis=1)
     token_weight = (response_mask.astype(F32) * SPAN / lengths).reshape(1, tokens)
+    weight_columns = lax.dynamic_slice_in_dim(student_weight, (1 - core) * half_width, half_width, 1)
+    blocks, (scalars, core_scalar, token_weight, ids, weight_theirs) = gather_tokens(
+        kept, (scalars, core_scalar, token_weight, token_ids.reshape(1, tokens), weight_columns)
+    )
 
     student_logits, teacher_logits, stats, hidden = pl.pallas_call(
         functools.partial(logits_kernel, half),
-        in_specs=[IN_SMEM] + [IN_HBM] * 18 + [IN_VMEM],
-        out_specs=[IN_HBM] * 4,
+        in_specs=[IN_SMEM] + [IN_VMEM] * 16 + [IN_HBM] * 2 + [IN_VMEM],
+        out_specs=[IN_HBM] * 2 + [IN_VMEM, IN_HBM],
         out_shape=[
             jax.ShapeDtypeStruct((head_rows, tokens), F32),
             jax.ShapeDtypeStruct((head_rows, tokens), F32),
@@ -350,19 +383,27 @@
             pltpu.VMEM((head_rows, width_t), BF16),
             pltpu.VMEM((head_rows, tokens), F32),
             pltpu.VMEM((head_rows, tokens), F32),
-            pltpu.VMEM((64, 2, 8, 128), F32),
             pltpu.SemaphoreType.DMA((2, 15)),
             pltpu.SemaphoreType.DMA((2, 5)),
         ],
-        compiler_params=params(),
+        compiler_params=params(42 * 1024 * 1024),
         cost_estimate=pl.CostEstimate(
             flops=2 * head_rows * tokens * (width + width_t), bytes_accessed=24_000_000, transcendentals=2 * head_rows * tokens
         ),
-    )(scalars, student_hidden, teacher_hidden, *blocks, student_weight, teacher_weight, token_ids.reshape(1, tokens))
-
-    stats, (student_logits, teacher_logits) = lax.optimization_barrier((stats, (student_logits, teacher_logits)))
+    )(scalars, student_hidden, teacher_hidden, *blocks, student_weight, teacher_weight, ids)
+
     student_theirs, teacher_theirs = swap([student_logits, teacher_logits])
     every = lax.all_to_all(stats.reshape(128, 8, 128), BOTH, split_axis=0, concat_axis=0, tiled=True)
+    both_s, both_t = pl.pallas_call(
+        join_kernel,
+        in_specs=[IN_HBM] * 4,
+        out_specs=[IN_HBM] * 2,
+        out_shape=[jax.ShapeDtypeStruct((2 * head_rows, tokens), F32)] * 2,
+        scratch_shapes=[pltpu.VMEM((2, 2 * head_rows, tokens), F32), pltpu.SemaphoreType.DMA((6,))],
+        compiler_params=params(),
+        cost_estimate=pl.CostEstimate(flops=0, bytes_accessed=11_000_000, transcendentals=0),
+    )(student_logits, teacher_logits, student_theirs, teacher_theirs)
+    every, both_s, both_t = lax.optimization_barrier((every, both_s, both_t))
     mine = pl.pallas_call(
         combine_kernel,
         in_specs=[IN_VMEM],
@@ -375,7 +416,7 @@
     groups, quarter = tokens // 16, half_width // 2
     share, grad_t = pl.pallas_call(
         share_kernel,
-        in_specs=[IN_SMEM] + [IN_HBM] * 2 + [IN_VMEM] + [IN_HBM] * 6,
+        in_specs=[IN_SMEM] + [IN_HBM] * 2 + [IN_VMEM] + [IN_HBM] * 4,
         out_specs=[IN_HBM, IN_HBM],
         out_shape=[
             jax.ShapeDtypeStruct((groups, 2, 16, quarter), BF16),
@@ -390,13 +431,12 @@
             pltpu.VMEM((head_rows, tokens), BF16),
             pltpu.VMEM((half_width // 512, 2 * head_rows, 512), BF16),
             pltpu.VMEM((groups, 2, 16, quarter), BF16),
-            pltpu.SemaphoreType.DMA((8, 5)),
+            pltpu.SemaphoreType.DMA((8, 10)),
         ],
         compiler_params=params(),
         cost_estimate=pl.CostEstimate(flops=2 * head_rows * tokens * width, bytes_accessed=16_000_000, transcendentals=0),
     )(
-        core_scalar, mine, other, token_weight, student_logits, teacher_logits, student_theirs, teacher_theirs,
-        student_weight, weight_theirs,
+        core_scalar, mine, other, token_weight, both_s, both_t, student_weight, weight_theirs,
     )
     parts = lax.all_to_all(
         share.reshape(64, 16, quarter), BOTH, split_axis=0, concat_axis=0, tiled=True, axis_index_groups=SAME_CORE

time: 151 us -> 149 us (0.987)
  waiting for transfers between devices: 58.7 us -> 53.1 us
  Pallas kernels: 33.1 us -> 36.2 us
    all_to_all x1, waiting for transfers between devices: 13.6 us -> 9.47 us  [shards(): lax.all_to_all(stats.reshape(128, 8, 128), BOTH, split_axis=0, concat_axi...]
    pallas_call x0 -> x1, Pallas kernels: none -> 4.07 us  [shards(): pl.pallas_call(join_kernel, in_specs=[IN_HBM] * 4, out_specs=[IN_HBM] * 2...]
    ppermute x19, waiting for transfers between devices: 21 us -> 19.5 us  [send(): return lax.ppermute(value, BOTH, where)]
    unnamed x44 -> x20, local copies, waits for them, and re-layouts: 3.95 us -> 3.54 us
  transfers between devices with their start and end apart: 21 -> 21, of which waited for: 14 -> 14; matrix products, arithmetic and copies ran while one was open for 4% -> 5% of each run, Pallas kernels for 14% -> 16%
where the time goes in v2:
time: 149 us
  waiting for transfers between devices  53.1 us (36%)
  Pallas kernels  36.2 us (24%)
  starting transfers between devices  34.4 us (23%)
  blocking collectives  13 us (9%)
  local copies, waits for them, and re-layouts  8.77 us (6%)
  other arithmetic  2.3 us (2%)
    ppermute x19, starting transfers between devices, send(): return lax.ppermute(value, BOTH, where)  25.5 us
    all_to_all x1, waiting for transfers between devices, shards(): lax.all_to_all(share.reshape(64, 16, quarter), BOTH, split_axis=0, concat...  24.1 us
    ppermute x19, waiting for transfers between devices, send(): return lax.ppermute(value, BOTH, where)  19.5 us
    all_to_all x1, blocking collectives, shards(): lax.all_to_all(summed, BOTH, split_axis=0, concat_axis=0, tiled=True, axi...  13 us
    pallas_call x1, Pallas kernels, shards(): pl.pallas_call(functools.partial(logits_kernel, half), in_specs=[IN_SMEM]...  12.9 us
    pallas_call x1, Pallas kernels, shards(): pl.pallas_call(share_kernel, in_specs=[IN_SMEM] + [IN_HBM] * 2 + [IN_VMEM...  9.82 us
    all_to_all x1, waiting for transfers between devices, shards(): lax.all_to_all(stats.reshape(128, 8, 128), BOTH, split_axis=0, concat_axi...  9.47 us
    pallas_call x1, Pallas kernels, shards(): pl.pallas_call(grad_weight_kernel, grid=(width // 1024,), in_specs=[pl.Bl...  5.93 us
  transfers between devices with their start and end apart: 21, of which 14 were waited for; matrix products, arithmetic and copies ran while one was open for 5% of the time, Pallas kernels for 16%

profile of v2, /device:TPU:1, one launch (start us, length us, event | category | flops | bytes accessed | tf_op | source)
XLA Modules:
  0.0 148.6 jit_solution(12446420186959565505)
XLA Ops:
  0.7 1.9 %shard_map.102 = bf16[32,9216]{1,0:T(8,128)(2,1)} custom-call(s32[1]{0:T(128)} %bitcast.scalars, bf16[64,5120]{1,0:T(8,128)(2,1)} %own_s.1, bf16[64,4096]{1,0:T(8,128)(2,1)} %own_t.1), custom_call_target="tpu_custom_call" | custom-call | tf_op jit(solution)/shard_map/pallas_call | solution.py:353
  2.6 4.7 %collective-permute-start = (bf16[32,9216]{1,0:T(8,128)(2,1)}, bf16[32,9216]{1,0:T(8,128)(2,1)S(1)}, u32[]{:S(2)}, u32[]{:S(2)}) collective-permute-start(bf16[32,9216]{1,0:T(8,128)(2,1)} %shard_map.102), channel_id=1, source_target_pairs={{0,16},{1,49},{2,18},{3,51},{4,20},{5,53},{6,22},{7,55},{8,24},{9,... | collective-permute-start | bytes 1769480 | tf_op jit(solution)/shard_map/ppermute | solution.py:48
  7.2 2.5 %collective-permute-start.1 = (bf16[32,9216]{1,0:T(8,128)(2,1)}, bf16[32,9216]{1,0:T(8,128)(2,1)S(1)}, u32[]{:S(2)}, u32[]{:S(2)}) collective-permute-start(bf16[32,9216]{1,0:T(8,128)(2,1)} %shard_map.102), channel_id=1, source_target_pairs={{0,64},{1,67},{2,66},{3,65},{4,68},{5,71},{6,70},{7,69},{8,72},{9,... | collective-permute-start | bytes 1769480 | tf_op jit(solution)/shard_map/ppermute | solution.py:48
  12.1 3.9 %constant_dynamic-slice_fusion = bf16[640,2560]{1,0:T(8,128)(2,1)} fusion(bf16[640,5120]{1,0:T(8,128)(2,1)} %weight_mine.1, s32[]{:T(128)S(6)} %select_n.88), kind=kLoop, calls=%fused_computation.6 | loop fusion | bytes 6553604 | tf_op jit(solution)/shard_map/dynamic_slice | solution.py:364
  16.9 3.0 %collective-permute-start.2 = (bf16[32,9216]{1,0:T(8,128)(2,1)S(1)}, bf16[32,9216]{1,0:T(8,128)(2,1)S(1)}, u32[]{:S(2)}, u32[]{:S(2)}) collective-permute-start(bf16[32,9216]{1,0:T(8,128)(2,1)S(1)} %collective-permute-done.refs_0_), channel_id=1, source_target_pairs={{0,64},{1,67},{2,66},{3,65},{4,68},{5,71},{6,70},{7,69},{8,72},{9,... | collective-permute-start | bytes 1769480 | tf_op jit(solution)/shard_map/ppermute | solution.py:48
  20.0 2.7 %collective-permute-start.4 = (bf16[32,9216]{1,0:T(8,128)(2,1)S(1)}, bf16[32,9216]{1,0:T(8,128)(2,1)S(1)}, u32[]{:S(2)}, u32[]{:S(2)}) collective-permute-start(bf16[32,9216]{1,0:T(8,128)(2,1)S(1)} %collective-permute-done.refs_0_), channel_id=1, source_target_pairs={{0,4},{1,13},{2,6},{3,15},{4,8},{5,1},{6,10},{7,3},{8,12},{9,5},{1... | collective-permute-start | bytes 1769480 | tf_op jit(solution)/shard_map/ppermute | solution.py:48
  23.2 3.5 %collective-permute-done.2.refs_4_ = bf16[32,9216]{1,0:T(8,128)(2,1)S(1)} collective-permute-done((bf16[32,9216]{1,0:T(8,128)(2,1)S(1)}, bf16[32,9216]{1,0:T(8,128)(2,1)S(1)}, u32[]{:S(2)}, u32[]{:S(2)}) %collective-permute-start.2) | collective-permute-done | bytes 589856 | tf_op jit(solution)/shard_map/ppermute | solution.py:48
  26.7 2.2 %collective-permute-done.3.refs_3_ = bf16[32,9216]{1,0:T(8,128)(2,1)S(1)} collective-permute-done((bf16[32,9216]{1,0:T(8,128)(2,1)S(1)}, bf16[32,9216]{1,0:T(8,128)(2,1)S(1)}, u32[]{:S(2)}, u32[]{:S(2)}) %collective-permute-start.3) | collective-permute-done | bytes 589856 | tf_op jit(solution)/shard_map/ppermute | solution.py:48
  30.7 2.7 %collective-permute-start.7 = (bf16[32,9216]{1,0:T(8,128)(2,1)S(1)}, bf16[32,9216]{1,0:T(8,128)(2,1)S(1)}, u32[]{:S(2)}, u32[]{:S(2)}) collective-permute-start(bf16[32,9216]{1,0:T(8,128)(2,1)S(1)} %collective-permute-done.3.refs_3_), channel_id=1, source_target_pairs={{0,64},{1,67},{2,66},{3,65},{4,68},{5,71},{6,70},{7,69},{8,72},{9,... | collective-permute-start | bytes 1769480 | tf_op jit(solution)/shard_map/ppermute | solution.py:48
  35.4 4.8 %collective-permute-done.7.refs_6_ = bf16[32,9216]{1,0:T(8,128)(2,1)S(1)} collective-permute-done((bf16[32,9216]{1,0:T(8,128)(2,1)S(1)}, bf16[32,9216]{1,0:T(8,128)(2,1)S(1)}, u32[]{:S(2)}, u32[]{:S(2)}) %collective-permute-start.7) | collective-permute-done | bytes 589856 | tf_op jit(solution)/shard_map/ppermute | solution.py:48
  40.2 2.2 %collective-permute-done.8.refs_5_ = bf16[32,9216]{1,0:T(8,128)(2,1)S(1)} collective-permute-done((bf16[32,9216]{1,0:T(8,128)(2,1)S(1)}, bf16[32,9216]{1,0:T(8,128)(2,1)S(1)}, u32[]{:S(2)}, u32[]{:S(2)}) %collective-permute-start.8) | collective-permute-done | bytes 589856 | tf_op jit(solution)/shard_map/ppermute | solution.py:48
  42.4 2.6 %collective-permute-start.12 = (bf16[32,9216]{1,0:T(8,128)(2,1)S(1)}, bf16[32,9216]{1,0:T(8,128)(2,1)S(1)}, u32[]{:S(2)}, u32[]{:S(2)}) collective-permute-start(bf16[32,9216]{1,0:T(8,128)(2,1)S(1)} %collective-permute-done.8.refs_5_), channel_id=1, source_target_pairs={{0,1},{1,0},{2,3},{3,2},{4,5},{5,4},{6,7},{7,6},{8,9},{9,8},{10,11... | collective-permute-start | bytes 1769480 | tf_op jit(solution)/shard_map/ppermute | solution.py:48
  45.0 1.6 %collective-permute-done.12.refs_12_ = bf16[32,9216]{1,0:T(8,128)(2,1)S(1)} collective-permute-done((bf16[32,9216]{1,0:T(8,128)(2,1)S(1)}, bf16[32,9216]{1,0:T(8,128)(2,1)S(1)}, u32[]{:S(2)}, u32[]{:S(2)}) %collective-permute-start.12) | collective-permute-done | bytes 589856 | tf_op jit(solution)/shard_map/ppermute | solution.py:48
  47.8 12.9 %shard_map.103 = (f32[640,512]{1,0:T(8,128)S(1)}, f32[640,512]{1,0:T(8,128)}, f32[64,2,8,128]{3,2,1,0:T(8,128)}, bf16[512,5120]{1,0:T(8,128)(2,1)}) custom-call(s32[16]{0:T(128)S(1)} %stack.67.scalars, bf16[64,5120]{1,0:T(8,128)(2,1)S(1)} %copy-done.3, bf16[64,4096]{1,0:T(8,128)(2,1)S(1)} %copy-done.4, bf16[32,9216]{1,0:T(8,128)(2,1)S(1)} %collective-permute-done.refs_0_, ...), custom_call_target="tpu_custom_call" | custom-call | flops 6039797760 | bytes 24000000 | tf_op jit(solution)/shard_map/pallas_call | solution.py:369
  61.8 4.0 %all-to-all-start = ((f32[128,8,128]{2,1,0:T(8,128)}), f32[128,8,128]{2,1,0:T(8,128)S(1)}, u32[]{:S(2)}, u32[]{:S(2)}) async-start(f32[128,8,128]{2,1,0:T(8,128)} %bitcast.20), calls=%async_computation | async-start | bytes 1048576 | tf_op jit(solution)/shard_map/all_to_all | solution.py:396
  66.1 4.1 %shard_map.104 = (f32[1280,512]{1,0:T(8,128)}, f32[1280,512]{1,0:T(8,128)}) custom-call(f32[640,512]{1,0:T(8,128)} %copy-done.1, f32[640,512]{1,0:T(8,128)} %get-tuple-element.59.t_mine, f32[640,512]{1,0:T(8,128)} %collective-permute-done.14.s_theirs, f32[640,512]{1,0:T(8,128)} %collective-permute-done.15.t_theirs), custom_call_target="tpu_custom_call" | custom-call | bytes 11000000 | tf_op jit(solution)/shard_map/pallas_call | solution.py:397
  70.2 9.5 %all-to-all-done.every = f32[128,8,128]{2,1,0:T(8,128)S(1)} async-done(((f32[128,8,128]{2,1,0:T(8,128)}), f32[128,8,128]{2,1,0:T(8,128)S(1)}, u32[]{:S(2)}, u32[]{:S(2)}) %all-to-all-start) | async-done | bytes 524320 | tf_op jit(solution)/shard_map/all_to_all | solution.py:396
  82.1 9.8 %shard_map.106 = (bf16[32,2,16,1280]{3,2,1,0:T(8,128)(2,1)}, bf16[640,512]{1,0:T(8,128)(2,1)}) custom-call(s32[1]{0:T(128)} %bitcast.17.scalars, f32[8,128]{1,0:T(8,128)} %copy-done.5, f32[8,128]{1,0:T(8,128)} %copy-done.8, f32[1,512]{1,0:T(1,128)} %bitcast.28, f32[1280,512]{1,0:T(8,128)} %get-tuple-element.64.student, ...), custom_call_target="tpu_custom_call" | custom-call | flops 3355443200 | bytes 16000000 | tf_op jit(solution)/shard_map/pallas_call | solution.py:417
  92.0 4.9 %all-to-all-start.1 = ((bf16[64,16,1280]{2,1,0:T(8,128)(2,1)}), bf16[64,16,1280]{2,1,0:T(8,128)(2,1)S(1)}, u32[]{:S(2)}, u32[]{:S(2)}) async-start(bf16[64,16,1280]{2,1,0:T(8,128)(2,1)} %bitcast.27), calls=%async_computation.1 | async-start | bytes 5242880 | tf_op jit(solution)/shard_map/all_to_all | solution.py:441
  98.1 2.5 %copy-done = bf16[512,5120]{1,0:T(8,128)(2,1)S(1)} copy-done((bf16[512,5120]{1,0:T(8,128)(2,1)S(1)}, bf16[512,5120]{1,0:T(8,128)(2,1)}, u32[]{:S(2)}) %copy-start) | copy-done | bytes 5242904
  100.6 5.9 %shard_map.107 = bf16[640,5120]{1,0:T(8,128)(2,1)} custom-call(bf16[640,512]{1,0:T(8,128)(2,1)S(1)} %copy-done.2, bf16[512,5120]{1,0:T(8,128)(2,1)S(1)} %copy-done), custom_call_target="tpu_custom_call" | custom-call | flops 3355443200 | bytes 13000000 | tf_op jit(solution)/shard_map/pallas_call | solution.py:445
  106.5 24.1 %all-to-all-done.1.parts = bf16[64,16,1280]{2,1,0:T(8,128)(2,1)S(1)} async-done(((bf16[64,16,1280]{2,1,0:T(8,128)(2,1)}), bf16[64,16,1280]{2,1,0:T(8,128)(2,1)S(1)}, u32[]{:S(2)}, u32[]{:S(2)}) %all-to-all-start.1) | async-done | bytes 2621472 | tf_op jit(solution)/shard_map/all_to_all | solution.py:441
  131.0 13.0 %all_to_all.15.mine = bf16[8,16,1280]{2,1,0:T(8,128)(2,1)S(1)} all-to-all(bf16[8,16,1280]{2,1,0:T(8,128)(2,1)S(1)} %shard_map.108), channel_id=1, replica_groups={{0,2,4,6,8,10,12,14},{1,3,5,7,9,11,13,15},{16,18,20,22,24,26,28,30},{17..., dimensions={0} | all-to-all | bytes 655360 | tf_op jit(solution)/shard_map/all_to_all | solution.py:471
  144.0 2.4 %collective-permute-start.18 = (bf16[8,16,1280]{2,1,0:T(8,128)(2,1)S(1)}, bf16[8,16,1280]{2,1,0:T(8,128)(2,1)S(1)}, u32[]{:S(2)}, u32[]{:S(2)}) collective-permute-start(bf16[8,16,1280]{2,1,0:T(8,128)(2,1)S(1)} %all_to_all.15.mine), channel_id=1, source_target_pairs={{0,1},{1,0},{2,3},{3,2},{4,5},{5,4},{6,7},{7,6},{8,9},{9,8},{10,11... | collective-permute-start | bytes 983048 | tf_op jit(solution)/shard_map/ppermute | solution.py:48
  (57 shorter events, 16.3 us)
Async XLA Ops:
  2.6 13.5 %collective-permute-start = (bf16[32,9216]{1,0:T(8,128)(2,1)}, bf16[32,9216]{1,0:T(8,128)(2,1)S(1)}, u32[]{:S(2)}, u32[]{:S(2)}) collective-permute-start(bf16[32,9216]{1,0:T(8,128)(2,1)} %shard_map.102), channel_id=1, source_target_pairs={{0,16},{1,49},{2,18},{3,51},{4,20},{5,53},{6,22},{7,55},{8,24},{9,... | collective-permute-start | bytes 1769480 | tf_op jit(solution)/shard_map/ppermute | solution.py:48
  7.2 9.6 %collective-permute-start.1 = (bf16[32,9216]{1,0:T(8,128)(2,1)}, bf16[32,9216]{1,0:T(8,128)(2,1)S(1)}, u32[]{:S(2)}, u32[]{:S(2)}) collective-permute-start(bf16[32,9216]{1,0:T(8,128)(2,1)} %shard_map.102), channel_id=1, source_target_pairs={{0,64},{1,67},{2,66},{3,65},{4,68},{5,71},{6,70},{7,69},{8,72},{9,... | collective-permute-start | bytes 1769480 | tf_op jit(solution)/shard_map/ppermute | solution.py:48
  12.1 35.7 %copy-start.3 = (bf16[64,5120]{1,0:T(8,128)(2,1)S(1)}, bf16[64,5120]{1,0:T(8,128)(2,1)}, u32[]{:S(2)}) copy-start(bf16[64,5120]{1,0:T(8,128)(2,1)} %own_s.1) | copy-start | bytes 1966084
  12.1 35.7 %copy-start.4 = (bf16[64,4096]{1,0:T(8,128)(2,1)S(1)}, bf16[64,4096]{1,0:T(8,128)(2,1)}, u32[]{:S(2)}) copy-start(bf16[64,4096]{1,0:T(8,128)(2,1)} %own_t.1) | copy-start | bytes 1572868
  12.1 35.7 %copy-start.7 = (s32[512]{0:T(512)S(1)}, s32[512]{0:T(512)}, u32[]{:S(2)}) copy-start(s32[512]{0:T(512)} %param.11) | copy-start | bytes 6148
  16.9 9.8 %collective-permute-start.2 = (bf16[32,9216]{1,0:T(8,128)(2,1)S(1)}, bf16[32,9216]{1,0:T(8,128)(2,1)S(1)}, u32[]{:S(2)}, u32[]{:S(2)}) collective-permute-start(bf16[32,9216]{1,0:T(8,128)(2,1)S(1)} %collective-permute-done.refs_0_), channel_id=1, source_target_pairs={{0,64},{1,67},{2,66},{3,65},{4,68},{5,71},{6,70},{7,69},{8,72},{9,... | collective-permute-start | bytes 1769480 | tf_op jit(solution)/shard_map/ppermute | solution.py:48
  19.9 9.0 %collective-permute-start.3 = (bf16[32,9216]{1,0:T(8,128)(2,1)S(1)}, bf16[32,9216]{1,0:T(8,128)(2,1)S(1)}, u32[]{:S(2)}, u32[]{:S(2)}) collective-permute-start(bf16[32,9216]{1,0:T(8,128)(2,1)S(1)} %collective-permute-done.refs_0_), channel_id=1, source_target_pairs={{0,16},{1,49},{2,18},{3,51},{4,20},{5,53},{6,22},{7,55},{8,24},{9,... | collective-permute-start | bytes 1769480 | tf_op jit(solution)/shard_map/ppermute | solution.py:48
  20.0 9.6 %collective-permute-start.4 = (bf16[32,9216]{1,0:T(8,128)(2,1)S(1)}, bf16[32,9216]{1,0:T(8,128)(2,1)S(1)}, u32[]{:S(2)}, u32[]{:S(2)}) collective-permute-start(bf16[32,9216]{1,0:T(8,128)(2,1)S(1)} %collective-permute-done.refs_0_), channel_id=1, source_target_pairs={{0,4},{1,13},{2,6},{3,15},{4,8},{5,1},{6,10},{7,3},{8,12},{9,5},{1... | collective-permute-start | bytes 1769480 | tf_op jit(solution)/shard_map/ppermute | solution.py:48
  22.7 6.8 %collective-permute-start.5 = (bf16[32,9216]{1,0:T(8,128)(2,1)S(1)}, bf16[32,9216]{1,0:T(8,128)(2,1)S(1)}, u32[]{:S(2)}, u32[]{:S(2)}) collective-permute-start(bf16[32,9216]{1,0:T(8,128)(2,1)S(1)} %collective-permute-done.refs_0_), channel_id=1, source_target_pairs={{0,1},{1,0},{2,3},{3,2},{4,5},{5,4},{6,7},{7,6},{8,9},{9,8},{10,11... | collective-permute-start | bytes 1769480 | tf_op jit(solution)/shard_map/ppermute | solution.py:48
  22.7 6.8 %collective-permute-start.6 = (bf16[32,9216]{1,0:T(8,128)(2,1)S(1)}, bf16[32,9216]{1,0:T(8,128)(2,1)S(1)}, u32[]{:S(2)}, u32[]{:S(2)}) collective-permute-start(bf16[32,9216]{1,0:T(8,128)(2,1)S(1)} %collective-permute-done.1.refs_2_), channel_id=1, source_target_pairs={{0,1},{1,0},{2,3},{3,2},{4,5},{5,4},{6,7},{7,6},{8,9},{9,8},{10,11... | collective-permute-start | bytes 1769480 | tf_op jit(solution)/shard_map/ppermute | solution.py:48
  29.6 5.3 %collective-permute-start.10 = (bf16[32,9216]{1,0:T(8,128)(2,1)S(1)}, bf16[32,9216]{1,0:T(8,128)(2,1)S(1)}, u32[]{:S(2)}, u32[]{:S(2)}) collective-permute-start(bf16[32,9216]{1,0:T(8,128)(2,1)S(1)} %collective-permute-done.3.refs_3_), channel_id=1, source_target_pairs={{0,1},{1,0},{2,3},{3,2},{4,5},{5,4},{6,7},{7,6},{8,9},{9,8},{10,11... | collective-permute-start | bytes 1769480 | tf_op jit(solution)/shard_map/ppermute | solution.py:48
  30.7 9.5 %collective-permute-start.7 = (bf16[32,9216]{1,0:T(8,128)(2,1)S(1)}, bf16[32,9216]{1,0:T(8,128)(2,1)S(1)}, u32[]{:S(2)}, u32[]{:S(2)}) collective-permute-start(bf16[32,9216]{1,0:T(8,128)(2,1)S(1)} %collective-permute-done.3.refs_3_), channel_id=1, source_target_pairs={{0,64},{1,67},{2,66},{3,65},{4,68},{5,71},{6,70},{7,69},{8,72},{9,... | collective-permute-start | bytes 1769480 | tf_op jit(solution)/shard_map/ppermute | solution.py:48
  33.3 2.0 %collective-permute-start.11 = (bf16[32,9216]{1,0:T(8,128)(2,1)S(1)}, bf16[32,9216]{1,0:T(8,128)(2,1)S(1)}, u32[]{:S(2)}, u32[]{:S(2)}) collective-permute-start(bf16[32,9216]{1,0:T(8,128)(2,1)S(1)} %collective-permute-done.4.refs_1_), channel_id=1, source_target_pairs={{0,1},{1,0},{2,3},{3,2},{4,5},{5,4},{6,7},{7,6},{8,9},{9,8},{10,11... | collective-permute-start | bytes 1769480 | tf_op jit(solution)/shard_map/ppermute | solution.py:48
  33.4 9.0 %collective-permute-start.8 = (bf16[32,9216]{1,0:T(8,128)(2,1)S(1)}, bf16[32,9216]{1,0:T(8,128)(2,1)S(1)}, u32[]{:S(2)}, u32[]{:S(2)}) collective-permute-start(bf16[32,9216]{1,0:T(8,128)(2,1)S(1)} %collective-permute-done.2.refs_4_), channel_id=1, source_target_pairs={{0,4},{1,13},{2,6},{3,15},{4,8},{5,1},{6,10},{7,3},{8,12},{9,5},{1... | collective-permute-start | bytes 1769480 | tf_op jit(solution)/shard_map/ppermute | solution.py:48
  34.9 7.5 %collective-permute-start.9 = (bf16[32,9216]{1,0:T(8,128)(2,1)S(1)}, bf16[32,9216]{1,0:T(8,128)(2,1)S(1)}, u32[]{:S(2)}, u32[]{:S(2)}) collective-permute-start(bf16[32,9216]{1,0:T(8,128)(2,1)S(1)} %collective-permute-done.2.refs_4_), channel_id=1, source_target_pairs={{0,1},{1,0},{2,3},{3,2},{4,5},{5,4},{6,7},{7,6},{8,9},{9,8},{10,11... | collective-permute-start | bytes 1769480 | tf_op jit(solution)/shard_map/ppermute | solution.py:48
  42.4 4.2 %collective-permute-start.12 = (bf16[32,9216]{1,0:T(8,128)(2,1)S(1)}, bf16[32,9216]{1,0:T(8,128)(2,1)S(1)}, u32[]{:S(2)}, u32[]{:S(2)}) collective-permute-start(bf16[32,9216]{1,0:T(8,128)(2,1)S(1)} %collective-permute-done.8.refs_5_), channel_id=1, source_target_pairs={{0,1},{1,0},{2,3},{3,2},{4,5},{5,4},{6,7},{7,6},{8,9},{9,8},{10,11... | collective-permute-start | bytes 1769480 | tf_op jit(solution)/shard_map/ppermute | solution.py:48
  45.0 2.5 %collective-permute-start.13 = (bf16[32,9216]{1,0:T(8,128)(2,1)S(1)}, bf16[32,9216]{1,0:T(8,128)(2,1)S(1)}, u32[]{:S(2)}, u32[]{:S(2)}) collective-permute-start(bf16[32,9216]{1,0:T(8,128)(2,1)S(1)} %collective-permute-done.7.refs_6_), channel_id=1, source_target_pairs={{0,1},{1,0},{2,3},{3,2},{4,5},{5,4},{6,7},{7,6},{8,9},{9,8},{10,11... | collective-permute-start | bytes 1769480 | tf_op jit(solution)/shard_map/ppermute | solution.py:48
  47.4 34.1 %collective-permute-start.17 = (bf16[640,2560]{1,0:T(8,128)(2,1)}, bf16[640,2560]{1,0:T(8,128)(2,1)}, u32[]{:S(2)}, u32[]{:S(2)}) collective-permute-start(bf16[640,2560]{1,0:T(8,128)(2,1)} %constant_dynamic-slice_fusion), channel_id=1, source_target_pairs={{0,1},{1,0},{2,3},{3,2},{4,5},{5,4},{6,7},{7,6},{8,9},{9,8},{10,11... | collective-permute-start | bytes 9830408 | tf_op jit(solution)/shard_map/ppermute | solution.py:48
  60.8 5.0 %collective-permute-start.14 = (f32[640,512]{1,0:T(8,128)S(1)}, f32[640,512]{1,0:T(8,128)}, u32[]{:S(2)}, u32[]{:S(2)}) collective-permute-start(f32[640,512]{1,0:T(8,128)S(1)} %get-tuple-element.58.s_mine), channel_id=1, source_target_pairs={{0,1},{1,0},{2,3},{3,2},{4,5},{5,4},{6,7},{7,6},{8,9},{9,8},{10,11... | collective-permute-start | bytes 3932168 | tf_op jit(solution)/shard_map/ppermute | solution.py:48
  61.0 5.1 %collective-permute-start.15 = (f32[640,512]{1,0:T(8,128)}, f32[640,512]{1,0:T(8,128)}, u32[]{:S(2)}, u32[]{:S(2)}) collective-permute-start(f32[640,512]{1,0:T(8,128)} %get-tuple-element.59.t_mine), channel_id=1, source_target_pairs={{0,1},{1,0},{2,3},{3,2},{4,5},{5,4},{6,7},{7,6},{8,9},{9,8},{10,11... | collective-permute-start | bytes 3932168 | tf_op jit(solution)/shard_map/ppermute | solution.py:48
  61.8 17.9 %all-to-all-start = ((f32[128,8,128]{2,1,0:T(8,128)}), f32[128,8,128]{2,1,0:T(8,128)S(1)}, u32[]{:S(2)}, u32[]{:S(2)}) async-start(f32[128,8,128]{2,1,0:T(8,128)} %bitcast.20), calls=%async_computation | async-start | bytes 1048576 | tf_op jit(solution)/shard_map/all_to_all | solution.py:396
  80.0 1.5 %collective-permute-start.16 = (f32[8,128]{1,0:T(8,128)S(1)}, f32[8,128]{1,0:T(8,128)S(1)}, u32[]{:S(2)}, u32[]{:S(2)}) collective-permute-start(f32[8,128]{1,0:T(8,128)S(1)} %shard_map.105.mine), channel_id=1, source_target_pairs={{0,1},{1,0},{2,3},{3,2},{4,5},{5,4},{6,7},{7,6},{8,9},{9,8},{10,11... | collective-permute-start | bytes 12296 | tf_op jit(solution)/shard_map/ppermute | solution.py:48
  92.0 38.7 %all-to-all-start.1 = ((bf16[64,16,1280]{2,1,0:T(8,128)(2,1)}), bf16[64,16,1280]{2,1,0:T(8,128)(2,1)S(1)}, u32[]{:S(2)}, u32[]{:S(2)}) async-start(bf16[64,16,1280]{2,1,0:T(8,128)(2,1)} %bitcast.27), calls=%async_computation.1 | async-start | bytes 5242880 | tf_op jit(solution)/shard_map/all_to_all | solution.py:441
  144.0 3.7 %collective-permute-start.18 = (bf16[8,16,1280]{2,1,0:T(8,128)(2,1)S(1)}, bf16[8,16,1280]{2,1,0:T(8,128)(2,1)S(1)}, u32[]{:S(2)}, u32[]{:S(2)}) collective-permute-start(bf16[8,16,1280]{2,1,0:T(8,128)(2,1)S(1)} %all_to_all.15.mine), channel_id=1, source_target_pairs={{0,1},{1,0},{2,3},{3,2},{4,5},{5,4},{6,7},{7,6},{8,9},{9,8},{10,11... | collective-permute-start | bytes 983048 | tf_op jit(solution)/shard_map/ppermute | solution.py:48
  (7 other events, 21.6 us)

commit v3 on v2

--- a/solution.py
+++ b/solution.py
@@ -61,10 +61,11 @@
     near_z, near_x, others = lax.optimization_barrier((send(kept, ALONG_Z), send(kept, ALONG_X), others))
     second = [send(near_z, ALONG_X), send(near_z, ALONG_Z), send(near_z, ALONG_Y)] + swap([near_z, near_x])
     near_zx, far_z, rest_z, o_near_z, o_near_x = lax.optimization_barrier(second)
-    third = [send(far_z, ALONG_X), send(near_zx, ALONG_Y)] + swap([near_zx, far_z, rest_z])
-    far_zx, rest_zx, o_near_zx, o_far_z, o_rest_z = lax.optimization_barrier(third)
+    far_zx, rest_zx = send(far_z, ALONG_X), send(near_zx, ALONG_Y)
+    far_zx, o_near_zx, o_far_z, rest_z = lax.optimization_barrier((far_zx, *swap([near_zx, far_z]), rest_z))
+    o_rest_z, o_far_zx, o_rest_zx = swap([rest_z, far_zx, rest_zx])
     scalars, core_scalar, token_weight, ids, weight_columns = others
-    o_rest_zx, o_far_zx, weight_columns = lax.optimization_barrier((*swap([rest_zx, far_zx]), weight_columns))
+    o_rest_z, o_far_zx, o_rest_zx, weight_columns = lax.optimization_barrier((o_rest_z, o_far_zx, o_rest_zx, weight_columns))
     weight_theirs = send(weight_columns, OTHER_CORE)
     mine = [near_z, rest_z, near_x, far_z, near_zx, rest_zx, far_zx]
     theirs = [o_near_z, o_rest_z, o_near_x, o_far_z, o_near_zx, o_rest_zx, o_far_zx]

time: 149 us -> 148 us (level)
  waiting for transfers between devices: 53.1 us -> 49.4 us
  starting transfers between devices: 34.4 us -> 37.3 us
    ppermute x19, waiting for transfers between devices: 19.5 us -> 15.5 us  [send(): return lax.ppermute(value, BOTH, where)]
    ppermute x19, starting transfers between devices: 25.5 us -> 27.1 us  [send(): return lax.ppermute(value, BOTH, where)]
  transfers between devices with their start and end apart: 21 -> 21, of which waited for: 14 -> 11; matrix products, arithmetic and copies ran while one was open for 5% -> 5% of each run, Pallas kernels for 16% -> 16%
where the time goes in v3:
time: 148 us
  waiting for transfers between devices  49.4 us (33%)
  starting transfers between devices  37.3 us (25%)
  Pallas kernels  36.2 us (24%)
  blocking collectives  13 us (9%)
  local copies, waits for them, and re-layouts  8.77 us (6%)
  other arithmetic  2.3 us (2%)
    ppermute x19, starting transfers between devices, send(): return lax.ppermute(value, BOTH, where)  27.1 us
    all_to_all x1, waiting for transfers between devices, shards(): lax.all_to_all(share.reshape(64, 16, quarter), BOTH, split_axis=0, concat...  24.1 us
    ppermute x19, waiting for transfers between devices, send(): return lax.ppermute(value, BOTH, where)  15.5 us
    all_to_all x1, blocking collectives, shards(): lax.all_to_all(summed, BOTH, split_axis=0, concat_axis=0, tiled=True, axi...  13 us
    pallas_call x1, Pallas kernels, shards(): pl.pallas_call(functools.partial(logits_kernel, half), in_specs=[IN_SMEM]...  12.9 us
    pallas_call x1, Pallas kernels, shards(): pl.pallas_call(share_kernel, in_specs=[IN_SMEM] + [IN_HBM] * 2 + [IN_VMEM...  9.82 us
    all_to_all x1, waiting for transfers between devices, shards(): lax.all_to_all(stats.reshape(128, 8, 128), BOTH, split_axis=0, concat_axi...  9.75 us
    pallas_call x1, Pallas kernels, shards(): pl.pallas_call(grad_weight_kernel, grid=(width // 1024,), in_specs=[pl.Bl...  5.94 us
  transfers between devices with their start and end apart: 21, of which 11 were waited for; matrix products, arithmetic and copies ran while one was open for 5% of the time, Pallas kernels for 16%

profile of v3, /device:TPU:1, one launch (start us, length us, event | category | flops | bytes accessed | tf_op | source)
XLA Modules:
  0.0 147.9 jit_solution(11665475274539775483)
XLA Ops:
  0.7 1.9 %shard_map.102 = bf16[32,9216]{1,0:T(8,128)(2,1)} custom-call(s32[1]{0:T(128)} %bitcast.scalars, bf16[64,5120]{1,0:T(8,128)(2,1)} %own_s.1, bf16[64,4096]{1,0:T(8,128)(2,1)} %own_t.1), custom_call_target="tpu_custom_call" | custom-call | tf_op jit(solution)/shard_map/pallas_call | solution.py:354
  2.6 4.7 %collective-permute-start = (bf16[32,9216]{1,0:T(8,128)(2,1)}, bf16[32,9216]{1,0:T(8,128)(2,1)S(1)}, u32[]{:S(2)}, u32[]{:S(2)}) collective-permute-start(bf16[32,9216]{1,0:T(8,128)(2,1)} %shard_map.102), channel_id=1, source_target_pairs={{0,16},{1,49},{2,18},{3,51},{4,20},{5,53},{6,22},{7,55},{8,24},{9,... | collective-permute-start | bytes 1769480 | tf_op jit(solution)/shard_map/ppermute | solution.py:48
  7.2 2.5 %collective-permute-start.1 = (bf16[32,9216]{1,0:T(8,128)(2,1)}, bf16[32,9216]{1,0:T(8,128)(2,1)S(1)}, u32[]{:S(2)}, u32[]{:S(2)}) collective-permute-start(bf16[32,9216]{1,0:T(8,128)(2,1)} %shard_map.102), channel_id=1, source_target_pairs={{0,64},{1,67},{2,66},{3,65},{4,68},{5,71},{6,70},{7,69},{8,72},{9,... | collective-permute-start | bytes 1769480 | tf_op jit(solution)/shard_map/ppermute | solution.py:48
  12.1 3.9 %constant_dynamic-slice_fusion = bf16[640,2560]{1,0:T(8,128)(2,1)} fusion(bf16[640,5120]{1,0:T(8,128)(2,1)} %weight_mine.1, s32[]{:T(128)S(6)} %select_n.88), kind=kLoop, calls=%fused_computation.6 | loop fusion | bytes 6553604 | tf_op jit(solution)/shard_map/dynamic_slice | solution.py:365
  16.9 3.0 %collective-permute-start.2 = (bf16[32,9216]{1,0:T(8,128)(2,1)S(1)}, bf16[32,9216]{1,0:T(8,128)(2,1)S(1)}, u32[]{:S(2)}, u32[]{:S(2)}) collective-permute-start(bf16[32,9216]{1,0:T(8,128)(2,1)S(1)} %collective-permute-done.refs_0_), channel_id=1, source_target_pairs={{0,64},{1,67},{2,66},{3,65},{4,68},{5,71},{6,70},{7,69},{8,72},{9,... | collective-permute-start | bytes 1769480 | tf_op jit(solution)/shard_map/ppermute | solution.py:48
  20.0 2.7 %collective-permute-start.4 = (bf16[32,9216]{1,0:T(8,128)(2,1)S(1)}, bf16[32,9216]{1,0:T(8,128)(2,1)S(1)}, u32[]{:S(2)}, u32[]{:S(2)}) collective-permute-start(bf16[32,9216]{1,0:T(8,128)(2,1)S(1)} %collective-permute-done.refs_0_), channel_id=1, source_target_pairs={{0,4},{1,13},{2,6},{3,15},{4,8},{5,1},{6,10},{7,3},{8,12},{9,5},{1... | collective-permute-start | bytes 1769480 | tf_op jit(solution)/shard_map/ppermute | solution.py:48
  23.2 3.5 %collective-permute-done.2.refs_4_ = bf16[32,9216]{1,0:T(8,128)(2,1)S(1)} collective-permute-done((bf16[32,9216]{1,0:T(8,128)(2,1)S(1)}, bf16[32,9216]{1,0:T(8,128)(2,1)S(1)}, u32[]{:S(2)}, u32[]{:S(2)}) %collective-permute-start.2) | collective-permute-done | bytes 589856 | tf_op jit(solution)/shard_map/ppermute | solution.py:48
  26.7 2.2 %collective-permute-done.3.refs_3_ = bf16[32,9216]{1,0:T(8,128)(2,1)S(1)} collective-permute-done((bf16[32,9216]{1,0:T(8,128)(2,1)S(1)}, bf16[32,9216]{1,0:T(8,128)(2,1)S(1)}, u32[]{:S(2)}, u32[]{:S(2)}) %collective-permute-start.3) | collective-permute-done | bytes 589856 | tf_op jit(solution)/shard_map/ppermute | solution.py:48
  30.2 2.0 %collective-permute-start.8 = (bf16[32,9216]{1,0:T(8,128)(2,1)S(1)}, bf16[32,9216]{1,0:T(8,128)(2,1)S(1)}, u32[]{:S(2)}, u32[]{:S(2)}) collective-permute-start(bf16[32,9216]{1,0:T(8,128)(2,1)S(1)} %collective-permute-done.2.refs_4_), channel_id=1, source_target_pairs={{0,1},{1,0},{2,3},{3,2},{4,5},{5,4},{6,7},{7,6},{8,9},{9,8},{10,11... | collective-permute-start | bytes 1769480 | tf_op jit(solution)/shard_map/ppermute | solution.py:48
  32.2 1.7 %collective-permute-start.10 = (bf16[32,9216]{1,0:T(8,128)(2,1)S(1)}, bf16[32,9216]{1,0:T(8,128)(2,1)S(1)}, u32[]{:S(2)}, u32[]{:S(2)}) collective-permute-start(bf16[32,9216]{1,0:T(8,128)(2,1)S(1)} %collective-permute-done.2.refs_4_), channel_id=1, source_target_pairs={{0,4},{1,13},{2,6},{3,15},{4,8},{5,1},{6,10},{7,3},{8,12},{9,5},{1... | collective-permute-start | bytes 1769480 | tf_op jit(solution)/shard_map/ppermute | solution.py:48
  33.9 4.7 %collective-permute-done.7.refs_6_ = bf16[32,9216]{1,0:T(8,128)(2,1)S(1)} collective-permute-done((bf16[32,9216]{1,0:T(8,128)(2,1)S(1)}, bf16[32,9216]{1,0:T(8,128)(2,1)S(1)}, u32[]{:S(2)}, u32[]{:S(2)}) %collective-permute-start.7) | collective-permute-done | bytes 589856 | tf_op jit(solution)/shard_map/ppermute | solution.py:48
  38.6 3.2 %collective-permute-start.11 = (bf16[32,9216]{1,0:T(8,128)(2,1)S(1)}, bf16[32,9216]{1,0:T(8,128)(2,1)S(1)}, u32[]{:S(2)}, u32[]{:S(2)}) collective-permute-start(bf16[32,9216]{1,0:T(8,128)(2,1)S(1)} %collective-permute-done.4.refs_1_), channel_id=1, source_target_pairs={{0,1},{1,0},{2,3},{3,2},{4,5},{5,4},{6,7},{7,6},{8,9},{9,8},{10,11... | collective-permute-start | bytes 1769480 | tf_op jit(solution)/shard_map/ppermute | solution.py:48
  41.9 1.9 %collective-permute-start.13 = (bf16[32,9216]{1,0:T(8,128)(2,1)S(1)}, bf16[32,9216]{1,0:T(8,128)(2,1)S(1)}, u32[]{:S(2)}, u32[]{:S(2)}) collective-permute-start(bf16[32,9216]{1,0:T(8,128)(2,1)S(1)} %collective-permute-done.10.refs_5_), channel_id=1, source_target_pairs={{0,1},{1,0},{2,3},{3,2},{4,5},{5,4},{6,7},{7,6},{8,9},{9,8},{10,11... | collective-permute-start | bytes 1769480 | tf_op jit(solution)/shard_map/ppermute | solution.py:48
  45.8 12.9 %shard_map.103 = (f32[640,512]{1,0:T(8,128)S(1)}, f32[640,512]{1,0:T(8,128)}, f32[64,2,8,128]{3,2,1,0:T(8,128)}, bf16[512,5120]{1,0:T(8,128)(2,1)}) custom-call(s32[16]{0:T(128)S(1)} %stack.67.scalars, bf16[64,5120]{1,0:T(8,128)(2,1)S(1)} %copy-done.3, bf16[64,4096]{1,0:T(8,128)(2,1)S(1)} %copy-done.4, bf16[32,9216]{1,0:T(8,128)(2,1)S(1)} %collective-permute-done.refs_0_, ...), custom_call_target="tpu_custom_call" | custom-call | flops 6039797760 | bytes 24000000 | tf_op jit(solution)/shard_map/pallas_call | solution.py:370
  59.8 5.4 %all-to-all-start = ((f32[128,8,128]{2,1,0:T(8,128)}), f32[128,8,128]{2,1,0:T(8,128)S(1)}, u32[]{:S(2)}, u32[]{:S(2)}) async-start(f32[128,8,128]{2,1,0:T(8,128)} %bitcast.20), calls=%async_computation | async-start | bytes 1048576 | tf_op jit(solution)/shard_map/all_to_all | solution.py:397
  65.1 4.1 %shard_map.104 = (f32[1280,512]{1,0:T(8,128)}, f32[1280,512]{1,0:T(8,128)}) custom-call(f32[640,512]{1,0:T(8,128)} %copy-done.1, f32[640,512]{1,0:T(8,128)} %get-tuple-element.59.t_mine, f32[640,512]{1,0:T(8,128)} %collective-permute-done.14.s_theirs, f32[640,512]{1,0:T(8,128)} %collective-permute-done.15.t_theirs), custom_call_target="tpu_custom_call" | custom-call | bytes 11000000 | tf_op jit(solution)/shard_map/pallas_call | solution.py:398
  69.2 9.8 %all-to-all-done.every = f32[128,8,128]{2,1,0:T(8,128)S(1)} async-done(((f32[128,8,128]{2,1,0:T(8,128)}), f32[128,8,128]{2,1,0:T(8,128)S(1)}, u32[]{:S(2)}, u32[]{:S(2)}) %all-to-all-start) | async-done | bytes 524320 | tf_op jit(solution)/shard_map/all_to_all | solution.py:397
  81.5 9.8 %shard_map.106 = (bf16[32,2,16,1280]{3,2,1,0:T(8,128)(2,1)}, bf16[640,512]{1,0:T(8,128)(2,1)}) custom-call(s32[1]{0:T(128)} %bitcast.17.scalars, f32[8,128]{1,0:T(8,128)} %copy-done.5, f32[8,128]{1,0:T(8,128)} %copy-done.8, f32[1,512]{1,0:T(1,128)} %bitcast.28, f32[1280,512]{1,0:T(8,128)} %get-tuple-element.64.student, ...), custom_call_target="tpu_custom_call" | custom-call | flops 3355443200 | bytes 16000000 | tf_op jit(solution)/shard_map/pallas_call | solution.py:418
  91.3 4.9 %all-to-all-start.1 = ((bf16[64,16,1280]{2,1,0:T(8,128)(2,1)}), bf16[64,16,1280]{2,1,0:T(8,128)(2,1)S(1)}, u32[]{:S(2)}, u32[]{:S(2)}) async-start(bf16[64,16,1280]{2,1,0:T(8,128)(2,1)} %bitcast.27), calls=%async_computation.1 | async-start | bytes 5242880 | tf_op jit(solution)/shard_map/all_to_all | solution.py:442
  97.4 2.5 %copy-done = bf16[512,5120]{1,0:T(8,128)(2,1)S(1)} copy-done((bf16[512,5120]{1,0:T(8,128)(2,1)S(1)}, bf16[512,5120]{1,0:T(8,128)(2,1)}, u32[]{:S(2)}) %copy-start) | copy-done | bytes 5242904
  99.9 5.9 %shard_map.107 = bf16[640,5120]{1,0:T(8,128)(2,1)} custom-call(bf16[640,512]{1,0:T(8,128)(2,1)S(1)} %copy-done.2, bf16[512,5120]{1,0:T(8,128)(2,1)S(1)} %copy-done), custom_call_target="tpu_custom_call" | custom-call | flops 3355443200 | bytes 13000000 | tf_op jit(solution)/shard_map/pallas_call | solution.py:446
  105.9 24.1 %all-to-all-done.1.parts = bf16[64,16,1280]{2,1,0:T(8,128)(2,1)S(1)} async-done(((bf16[64,16,1280]{2,1,0:T(8,128)(2,1)}), bf16[64,16,1280]{2,1,0:T(8,128)(2,1)S(1)}, u32[]{:S(2)}, u32[]{:S(2)}) %all-to-all-start.1) | async-done | bytes 2621472 | tf_op jit(solution)/shard_map/all_to_all | solution.py:442
  130.3 13.0 %all_to_all.15.mine = bf16[8,16,1280]{2,1,0:T(8,128)(2,1)S(1)} all-to-all(bf16[8,16,1280]{2,1,0:T(8,128)(2,1)S(1)} %shard_map.108), channel_id=1, replica_groups={{0,2,4,6,8,10,12,14},{1,3,5,7,9,11,13,15},{16,18,20,22,24,26,28,30},{17..., dimensions={0} | all-to-all | bytes 655360 | tf_op jit(solution)/shard_map/all_to_all | solution.py:472
  143.3 2.4 %collective-permute-start.18 = (bf16[8,16,1280]{2,1,0:T(8,128)(2,1)S(1)}, bf16[8,16,1280]{2,1,0:T(8,128)(2,1)S(1)}, u32[]{:S(2)}, u32[]{:S(2)}) collective-permute-start(bf16[8,16,1280]{2,1,0:T(8,128)(2,1)S(1)} %all_to_all.15.mine), channel_id=1, source_target_pairs={{0,1},{1,0},{2,3},{3,2},{4,5},{5,4},{6,7},{7,6},{8,9},{9,8},{10,11... | collective-permute-start | bytes 983048 | tf_op jit(solution)/shard_map/ppermute | solution.py:48
  (57 shorter events, 14.4 us)
Async XLA Ops:
  2.6 13.5 %collective-permute-start = (bf16[32,9216]{1,0:T(8,128)(2,1)}, bf16[32,9216]{1,0:T(8,128)(2,1)S(1)}, u32[]{:S(2)}, u32[]{:S(2)}) collective-permute-start(bf16[32,9216]{1,0:T(8,128)(2,1)} %shard_map.102), channel_id=1, source_target_pairs={{0,16},{1,49},{2,18},{3,51},{4,20},{5,53},{6,22},{7,55},{8,24},{9,... | collective-permute-start | bytes 1769480 | tf_op jit(solution)/shard_map/ppermute | solution.py:48
  7.2 9.6 %collective-permute-start.1 = (bf16[32,9216]{1,0:T(8,128)(2,1)}, bf16[32,9216]{1,0:T(8,128)(2,1)S(1)}, u32[]{:S(2)}, u32[]{:S(2)}) collective-permute-start(bf16[32,9216]{1,0:T(8,128)(2,1)} %shard_map.102), channel_id=1, source_target_pairs={{0,64},{1,67},{2,66},{3,65},{4,68},{5,71},{6,70},{7,69},{8,72},{9,... | collective-permute-start | bytes 1769480 | tf_op jit(solution)/shard_map/ppermute | solution.py:48
  12.1 33.7 %copy-start.3 = (bf16[64,5120]{1,0:T(8,128)(2,1)S(1)}, bf16[64,5120]{1,0:T(8,128)(2,1)}, u32[]{:S(2)}) copy-start(bf16[64,5120]{1,0:T(8,128)(2,1)} %own_s.1) | copy-start | bytes 1966084
  12.1 33.7 %copy-start.4 = (bf16[64,4096]{1,0:T(8,128)(2,1)S(1)}, bf16[64,4096]{1,0:T(8,128)(2,1)}, u32[]{:S(2)}) copy-start(bf16[64,4096]{1,0:T(8,128)(2,1)} %own_t.1) | copy-start | bytes 1572868
  12.1 33.7 %copy-start.7 = (s32[512]{0:T(512)S(1)}, s32[512]{0:T(512)}, u32[]{:S(2)}) copy-start(s32[512]{0:T(512)} %param.11) | copy-start | bytes 6148
  16.9 9.8 %collective-permute-start.2 = (bf16[32,9216]{1,0:T(8,128)(2,1)S(1)}, bf16[32,9216]{1,0:T(8,128)(2,1)S(1)}, u32[]{:S(2)}, u32[]{:S(2)}) collective-permute-start(bf16[32,9216]{1,0:T(8,128)(2,1)S(1)} %collective-permute-done.refs_0_), channel_id=1, source_target_pairs={{0,64},{1,67},{2,66},{3,65},{4,68},{5,71},{6,70},{7,69},{8,72},{9,... | collective-permute-start | bytes 1769480 | tf_op jit(solution)/shard_map/ppermute | solution.py:48
  19.9 9.0 %collective-permute-start.3 = (bf16[32,9216]{1,0:T(8,128)(2,1)S(1)}, bf16[32,9216]{1,0:T(8,128)(2,1)S(1)}, u32[]{:S(2)}, u32[]{:S(2)}) collective-permute-start(bf16[32,9216]{1,0:T(8,128)(2,1)S(1)} %collective-permute-done.refs_0_), channel_id=1, source_target_pairs={{0,16},{1,49},{2,18},{3,51},{4,20},{5,53},{6,22},{7,55},{8,24},{9,... | collective-permute-start | bytes 1769480 | tf_op jit(solution)/shard_map/ppermute | solution.py:48
  20.0 9.6 %collective-permute-start.4 = (bf16[32,9216]{1,0:T(8,128)(2,1)S(1)}, bf16[32,9216]{1,0:T(8,128)(2,1)S(1)}, u32[]{:S(2)}, u32[]{:S(2)}) collective-permute-start(bf16[32,9216]{1,0:T(8,128)(2,1)S(1)} %collective-permute-done.refs_0_), channel_id=1, source_target_pairs={{0,4},{1,13},{2,6},{3,15},{4,8},{5,1},{6,10},{7,3},{8,12},{9,5},{1... | collective-permute-start | bytes 1769480 | tf_op jit(solution)/shard_map/ppermute | solution.py:48
  22.7 6.8 %collective-permute-start.5 = (bf16[32,9216]{1,0:T(8,128)(2,1)S(1)}, bf16[32,9216]{1,0:T(8,128)(2,1)S(1)}, u32[]{:S(2)}, u32[]{:S(2)}) collective-permute-start(bf16[32,9216]{1,0:T(8,128)(2,1)S(1)} %collective-permute-done.refs_0_), channel_id=1, source_target_pairs={{0,1},{1,0},{2,3},{3,2},{4,5},{5,4},{6,7},{7,6},{8,9},{9,8},{10,11... | collective-permute-start | bytes 1769480 | tf_op jit(solution)/shard_map/ppermute | solution.py:48
  22.7 6.8 %collective-permute-start.6 = (bf16[32,9216]{1,0:T(8,128)(2,1)S(1)}, bf16[32,9216]{1,0:T(8,128)(2,1)S(1)}, u32[]{:S(2)}, u32[]{:S(2)}) collective-permute-start(bf16[32,9216]{1,0:T(8,128)(2,1)S(1)} %collective-permute-done.1.refs_2_), channel_id=1, source_target_pairs={{0,1},{1,0},{2,3},{3,2},{4,5},{5,4},{6,7},{7,6},{8,9},{9,8},{10,11... | collective-permute-start | bytes 1769480 | tf_op jit(solution)/shard_map/ppermute | solution.py:48
  29.6 9.0 %collective-permute-start.7 = (bf16[32,9216]{1,0:T(8,128)(2,1)S(1)}, bf16[32,9216]{1,0:T(8,128)(2,1)S(1)}, u32[]{:S(2)}, u32[]{:S(2)}) collective-permute-start(bf16[32,9216]{1,0:T(8,128)(2,1)S(1)} %collective-permute-done.3.refs_3_), channel_id=1, source_target_pairs={{0,64},{1,67},{2,66},{3,65},{4,68},{5,71},{6,70},{7,69},{8,72},{9,... | collective-permute-start | bytes 1769480 | tf_op jit(solution)/shard_map/ppermute | solution.py:48
  30.2 8.4 %collective-permute-start.8 = (bf16[32,9216]{1,0:T(8,128)(2,1)S(1)}, bf16[32,9216]{1,0:T(8,128)(2,1)S(1)}, u32[]{:S(2)}, u32[]{:S(2)}) collective-permute-start(bf16[32,9216]{1,0:T(8,128)(2,1)S(1)} %collective-permute-done.2.refs_4_), channel_id=1, source_target_pairs={{0,1},{1,0},{2,3},{3,2},{4,5},{5,4},{6,7},{7,6},{8,9},{9,8},{10,11... | collective-permute-start | bytes 1769480 | tf_op jit(solution)/shard_map/ppermute | solution.py:48
  32.2 6.4 %collective-permute-start.9 = (bf16[32,9216]{1,0:T(8,128)(2,1)S(1)}, bf16[32,9216]{1,0:T(8,128)(2,1)S(1)}, u32[]{:S(2)}, u32[]{:S(2)}) collective-permute-start(bf16[32,9216]{1,0:T(8,128)(2,1)S(1)} %collective-permute-done.3.refs_3_), channel_id=1, source_target_pairs={{0,1},{1,0},{2,3},{3,2},{4,5},{5,4},{6,7},{7,6},{8,9},{9,8},{10,11... | collective-permute-start | bytes 1769480 | tf_op jit(solution)/shard_map/ppermute | solution.py:48
  32.2 9.7 %collective-permute-start.10 = (bf16[32,9216]{1,0:T(8,128)(2,1)S(1)}, bf16[32,9216]{1,0:T(8,128)(2,1)S(1)}, u32[]{:S(2)}, u32[]{:S(2)}) collective-permute-start(bf16[32,9216]{1,0:T(8,128)(2,1)S(1)} %collective-permute-done.2.refs_4_), channel_id=1, source_target_pairs={{0,4},{1,13},{2,6},{3,15},{4,8},{5,1},{6,10},{7,3},{8,12},{9,5},{1... | collective-permute-start | bytes 1769480 | tf_op jit(solution)/shard_map/ppermute | solution.py:48
  38.6 5.2 %collective-permute-start.11 = (bf16[32,9216]{1,0:T(8,128)(2,1)S(1)}, bf16[32,9216]{1,0:T(8,128)(2,1)S(1)}, u32[]{:S(2)}, u32[]{:S(2)}) collective-permute-start(bf16[32,9216]{1,0:T(8,128)(2,1)S(1)} %collective-permute-done.4.refs_1_), channel_id=1, source_target_pairs={{0,1},{1,0},{2,3},{3,2},{4,5},{5,4},{6,7},{7,6},{8,9},{9,8},{10,11... | collective-permute-start | bytes 1769480 | tf_op jit(solution)/shard_map/ppermute | solution.py:48
  41.8 2.5 %collective-permute-start.12 = (bf16[32,9216]{1,0:T(8,128)(2,1)S(1)}, bf16[32,9216]{1,0:T(8,128)(2,1)S(1)}, u32[]{:S(2)}, u32[]{:S(2)}) collective-permute-start(bf16[32,9216]{1,0:T(8,128)(2,1)S(1)} %collective-permute-done.7.refs_6_), channel_id=1, source_target_pairs={{0,1},{1,0},{2,3},{3,2},{4,5},{5,4},{6,7},{7,6},{8,9},{9,8},{10,11... | collective-permute-start | bytes 1769480 | tf_op jit(solution)/shard_map/ppermute | solution.py:48
  41.9 3.5 %collective-permute-start.13 = (bf16[32,9216]{1,0:T(8,128)(2,1)S(1)}, bf16[32,9216]{1,0:T(8,128)(2,1)S(1)}, u32[]{:S(2)}, u32[]{:S(2)}) collective-permute-start(bf16[32,9216]{1,0:T(8,128)(2,1)S(1)} %collective-permute-done.10.refs_5_), channel_id=1, source_target_pairs={{0,1},{1,0},{2,3},{3,2},{4,5},{5,4},{6,7},{7,6},{8,9},{9,8},{10,11... | collective-permute-start | bytes 1769480 | tf_op jit(solution)/shard_map/ppermute | solution.py:48
  45.4 35.5 %collective-permute-start.17 = (bf16[640,2560]{1,0:T(8,128)(2,1)}, bf16[640,2560]{1,0:T(8,128)(2,1)}, u32[]{:S(2)}, u32[]{:S(2)}) collective-permute-start(bf16[640,2560]{1,0:T(8,128)(2,1)} %constant_dynamic-slice_fusion), channel_id=1, source_target_pairs={{0,1},{1,0},{2,3},{3,2},{4,5},{5,4},{6,7},{7,6},{8,9},{9,8},{10,11... | collective-permute-start | bytes 9830408 | tf_op jit(solution)/shard_map/ppermute | solution.py:48
  58.7 6.4 %collective-permute-start.14 = (f32[640,512]{1,0:T(8,128)S(1)}, f32[640,512]{1,0:T(8,128)}, u32[]{:S(2)}, u32[]{:S(2)}) collective-permute-start(f32[640,512]{1,0:T(8,128)S(1)} %get-tuple-element.58.s_mine), channel_id=1, source_target_pairs={{0,1},{1,0},{2,3},{3,2},{4,5},{5,4},{6,7},{7,6},{8,9},{9,8},{10,11... | collective-permute-start | bytes 3932168 | tf_op jit(solution)/shard_map/ppermute | solution.py:48
  59.0 6.2 %collective-permute-start.15 = (f32[640,512]{1,0:T(8,128)}, f32[640,512]{1,0:T(8,128)}, u32[]{:S(2)}, u32[]{:S(2)}) collective-permute-start(f32[640,512]{1,0:T(8,128)} %get-tuple-element.59.t_mine), channel_id=1, source_target_pairs={{0,1},{1,0},{2,3},{3,2},{4,5},{5,4},{6,7},{7,6},{8,9},{9,8},{10,11... | collective-permute-start | bytes 3932168 | tf_op jit(solution)/shard_map/ppermute | solution.py:48
  59.8 19.2 %all-to-all-start = ((f32[128,8,128]{2,1,0:T(8,128)}), f32[128,8,128]{2,1,0:T(8,128)S(1)}, u32[]{:S(2)}, u32[]{:S(2)}) async-start(f32[128,8,128]{2,1,0:T(8,128)} %bitcast.20), calls=%async_computation | async-start | bytes 1048576 | tf_op jit(solution)/shard_map/all_to_all | solution.py:397
  79.4 1.5 %collective-permute-start.16 = (f32[8,128]{1,0:T(8,128)S(1)}, f32[8,128]{1,0:T(8,128)S(1)}, u32[]{:S(2)}, u32[]{:S(2)}) collective-permute-start(f32[8,128]{1,0:T(8,128)S(1)} %shard_map.105.mine), channel_id=1, source_target_pairs={{0,1},{1,0},{2,3},{3,2},{4,5},{5,4},{6,7},{7,6},{8,9},{9,8},{10,11... | collective-permute-start | bytes 12296 | tf_op jit(solution)/shard_map/ppermute | solution.py:48
  91.3 38.7 %all-to-all-start.1 = ((bf16[64,16,1280]{2,1,0:T(8,128)(2,1)}), bf16[64,16,1280]{2,1,0:T(8,128)(2,1)S(1)}, u32[]{:S(2)}, u32[]{:S(2)}) async-start(bf16[64,16,1280]{2,1,0:T(8,128)(2,1)} %bitcast.27), calls=%async_computation.1 | async-start | bytes 5242880 | tf_op jit(solution)/shard_map/all_to_all | solution.py:442
  143.3 3.7 %collective-permute-start.18 = (bf16[8,16,1280]{2,1,0:T(8,128)(2,1)S(1)}, bf16[8,16,1280]{2,1,0:T(8,128)(2,1)S(1)}, u32[]{:S(2)}, u32[]{:S(2)}) collective-permute-start(bf16[8,16,1280]{2,1,0:T(8,128)(2,1)S(1)} %all_to_all.15.mine), channel_id=1, source_target_pairs={{0,1},{1,0},{2,3},{3,2},{4,5},{5,4},{6,7},{7,6},{8,9},{9,8},{10,11... | collective-permute-start | bytes 983048 | tf_op jit(solution)/shard_map/ppermute | solution.py:48
  (7 other events, 21.6 us)

commit v4 on v3

--- a/solution.py
+++ b/solution.py
@@ -170,7 +170,6 @@
     start_all(loads[1])
     product(0, 1)
     keep = pltpu.make_async_copy(hidden_s, out_hidden, sems.at[1, 4])
-    keep.start()
     entry = lax.broadcasted_iota(I32, (out_s.shape[0], 128), 0) + scalars[15]
     for j, at in enumerate(tiles):
         s = logits_s[:, at]
@@ -178,8 +177,9 @@
         put(j, 0, top + jnp.log(jnp.sum(jnp.exp(s - top), axis=0, keepdims=True)))
         put(j, 3, jnp.sum(jnp.where(ids[:, at] == entry, s, 0.0), axis=0, keepdims=True))
     wait_all(placing[1])
+    wait_all(loads[1])
+    keep.start()
     for i in range(2):
-        loads[1][i].wait()
         product(1, i)
     for j, at in enumerate(tiles):
         t = logits_t[:, at]

time: 148 us -> 148 us (level)
  no operation moved by 1% of the time
where the time goes in v4:
time: 148 us
  waiting for transfers between devices  49.4 us (33%)
  starting transfers between devices  37.4 us (25%)
  Pallas kernels  36 us (24%)
  blocking collectives  13 us (9%)
  local copies, waits for them, and re-layouts  8.77 us (6%)
  other arithmetic  2.3 us (2%)
    ppermute x19, starting transfers between devices, send(): return lax.ppermute(value, BOTH, where)  27.1 us
    all_to_all x1, waiting for transfers between devices, shards(): lax.all_to_all(share.reshape(64, 16, quarter), BOTH, split_axis=0, concat...  24.1 us
    ppermute x19, waiting for transfers between devices, send(): return lax.ppermute(value, BOTH, where)  15.5 us
    all_to_all x1, blocking collectives, shards(): lax.all_to_all(summed, BOTH, split_axis=0, concat_axis=0, tiled=True, axi...  13 us
    pallas_call x1, Pallas kernels, shards(): pl.pallas_call(functools.partial(logits_kernel, half), in_specs=[IN_SMEM]...  12.7 us
    pallas_call x1, Pallas kernels, shards(): pl.pallas_call(share_kernel, in_specs=[IN_SMEM] + [IN_HBM] * 2 + [IN_VMEM...  9.82 us
    all_to_all x1, waiting for transfers between devices, shards(): lax.all_to_all(stats.reshape(128, 8, 128), BOTH, split_axis=0, concat_axi...  9.75 us
    pallas_call x1, Pallas kernels, shards(): pl.pallas_call(grad_weight_kernel, grid=(width // 1024,), in_specs=[pl.Bl...  5.94 us
  transfers between devices with their start and end apart: 21, of which 11 were waited for; matrix products, arithmetic and copies ran while one was open for 5% of the time, Pallas kernels for 16%

profile of v4, /device:TPU:1, one launch (start us, length us, event | category | flops | bytes accessed | tf_op | source)
XLA Modules:
  0.0 147.7 jit_solution(15296704765724225169)
XLA Ops:
  0.7 1.9 %shard_map.102 = bf16[32,9216]{1,0:T(8,128)(2,1)} custom-call(s32[1]{0:T(128)} %bitcast.scalars, bf16[64,5120]{1,0:T(8,128)(2,1)} %own_s.1, bf16[64,4096]{1,0:T(8,128)(2,1)} %own_t.1), custom_call_target="tpu_custom_call" | custom-call | tf_op jit(solution)/shard_map/pallas_call | solution.py:354
  2.6 4.7 %collective-permute-start = (bf16[32,9216]{1,0:T(8,128)(2,1)}, bf16[32,9216]{1,0:T(8,128)(2,1)S(1)}, u32[]{:S(2)}, u32[]{:S(2)}) collective-permute-start(bf16[32,9216]{1,0:T(8,128)(2,1)} %shard_map.102), channel_id=1, source_target_pairs={{0,16},{1,49},{2,18},{3,51},{4,20},{5,53},{6,22},{7,55},{8,24},{9,... | collective-permute-start | bytes 1769480 | tf_op jit(solution)/shard_map/ppermute | solution.py:48
  7.2 2.5 %collective-permute-start.1 = (bf16[32,9216]{1,0:T(8,128)(2,1)}, bf16[32,9216]{1,0:T(8,128)(2,1)S(1)}, u32[]{:S(2)}, u32[]{:S(2)}) collective-permute-start(bf16[32,9216]{1,0:T(8,128)(2,1)} %shard_map.102), channel_id=1, source_target_pairs={{0,64},{1,67},{2,66},{3,65},{4,68},{5,71},{6,70},{7,69},{8,72},{9,... | collective-permute-start | bytes 1769480 | tf_op jit(solution)/shard_map/ppermute | solution.py:48
  12.1 3.9 %constant_dynamic-slice_fusion = bf16[640,2560]{1,0:T(8,128)(2,1)} fusion(bf16[640,5120]{1,0:T(8,128)(2,1)} %weight_mine.1, s32[]{:T(128)S(6)} %select_n.88), kind=kLoop, calls=%fused_computation.6 | loop fusion | bytes 6553604 | tf_op jit(solution)/shard_map/dynamic_slice | solution.py:365
  16.9 3.0 %collective-permute-start.2 = (bf16[32,9216]{1,0:T(8,128)(2,1)S(1)}, bf16[32,9216]{1,0:T(8,128)(2,1)S(1)}, u32[]{:S(2)}, u32[]{:S(2)}) collective-permute-start(bf16[32,9216]{1,0:T(8,128)(2,1)S(1)} %collective-permute-done.refs_0_), channel_id=1, source_target_pairs={{0,64},{1,67},{2,66},{3,65},{4,68},{5,71},{6,70},{7,69},{8,72},{9,... | collective-permute-start | bytes 1769480 | tf_op jit(solution)/shard_map/ppermute | solution.py:48
  20.0 2.7 %collective-permute-start.4 = (bf16[32,9216]{1,0:T(8,128)(2,1)S(1)}, bf16[32,9216]{1,0:T(8,128)(2,1)S(1)}, u32[]{:S(2)}, u32[]{:S(2)}) collective-permute-start(bf16[32,9216]{1,0:T(8,128)(2,1)S(1)} %collective-permute-done.refs_0_), channel_id=1, source_target_pairs={{0,4},{1,13},{2,6},{3,15},{4,8},{5,1},{6,10},{7,3},{8,12},{9,5},{1... | collective-permute-start | bytes 1769480 | tf_op jit(solution)/shard_map/ppermute | solution.py:48
  23.2 3.5 %collective-permute-done.2.refs_4_ = bf16[32,9216]{1,0:T(8,128)(2,1)S(1)} collective-permute-done((bf16[32,9216]{1,0:T(8,128)(2,1)S(1)}, bf16[32,9216]{1,0:T(8,128)(2,1)S(1)}, u32[]{:S(2)}, u32[]{:S(2)}) %collective-permute-start.2) | collective-permute-done | bytes 589856 | tf_op jit(solution)/shard_map/ppermute | solution.py:48
  26.7 2.2 %collective-permute-done.3.refs_3_ = bf16[32,9216]{1,0:T(8,128)(2,1)S(1)} collective-permute-done((bf16[32,9216]{1,0:T(8,128)(2,1)S(1)}, bf16[32,9216]{1,0:T(8,128)(2,1)S(1)}, u32[]{:S(2)}, u32[]{:S(2)}) %collective-permute-start.3) | collective-permute-done | bytes 589856 | tf_op jit(solution)/shard_map/ppermute | solution.py:48
  30.2 2.0 %collective-permute-start.8 = (bf16[32,9216]{1,0:T(8,128)(2,1)S(1)}, bf16[32,9216]{1,0:T(8,128)(2,1)S(1)}, u32[]{:S(2)}, u32[]{:S(2)}) collective-permute-start(bf16[32,9216]{1,0:T(8,128)(2,1)S(1)} %collective-permute-done.2.refs_4_), channel_id=1, source_target_pairs={{0,1},{1,0},{2,3},{3,2},{4,5},{5,4},{6,7},{7,6},{8,9},{9,8},{10,11... | collective-permute-start | bytes 1769480 | tf_op jit(solution)/shard_map/ppermute | solution.py:48
  32.2 1.7 %collective-permute-start.10 = (bf16[32,9216]{1,0:T(8,128)(2,1)S(1)}, bf16[32,9216]{1,0:T(8,128)(2,1)S(1)}, u32[]{:S(2)}, u32[]{:S(2)}) collective-permute-start(bf16[32,9216]{1,0:T(8,128)(2,1)S(1)} %collective-permute-done.2.refs_4_), channel_id=1, source_target_pairs={{0,4},{1,13},{2,6},{3,15},{4,8},{5,1},{6,10},{7,3},{8,12},{9,5},{1... | collective-permute-start | bytes 1769480 | tf_op jit(solution)/shard_map/ppermute | solution.py:48
  33.9 4.7 %collective-permute-done.7.refs_6_ = bf16[32,9216]{1,0:T(8,128)(2,1)S(1)} collective-permute-done((bf16[32,9216]{1,0:T(8,128)(2,1)S(1)}, bf16[32,9216]{1,0:T(8,128)(2,1)S(1)}, u32[]{:S(2)}, u32[]{:S(2)}) %collective-permute-start.7) | collective-permute-done | bytes 589856 | tf_op jit(solution)/shard_map/ppermute | solution.py:48
  38.6 3.2 %collective-permute-start.11 = (bf16[32,9216]{1,0:T(8,128)(2,1)S(1)}, bf16[32,9216]{1,0:T(8,128)(2,1)S(1)}, u32[]{:S(2)}, u32[]{:S(2)}) collective-permute-start(bf16[32,9216]{1,0:T(8,128)(2,1)S(1)} %collective-permute-done.4.refs_1_), channel_id=1, source_target_pairs={{0,1},{1,0},{2,3},{3,2},{4,5},{5,4},{6,7},{7,6},{8,9},{9,8},{10,11... | collective-permute-start | bytes 1769480 | tf_op jit(solution)/shard_map/ppermute | solution.py:48
  41.9 1.9 %collective-permute-start.13 = (bf16[32,9216]{1,0:T(8,128)(2,1)S(1)}, bf16[32,9216]{1,0:T(8,128)(2,1)S(1)}, u32[]{:S(2)}, u32[]{:S(2)}) collective-permute-start(bf16[32,9216]{1,0:T(8,128)(2,1)S(1)} %collective-permute-done.10.refs_5_), channel_id=1, source_target_pairs={{0,1},{1,0},{2,3},{3,2},{4,5},{5,4},{6,7},{7,6},{8,9},{9,8},{10,11... | collective-permute-start | bytes 1769480 | tf_op jit(solution)/shard_map/ppermute | solution.py:48
  45.8 12.7 %shard_map.103 = (f32[640,512]{1,0:T(8,128)S(1)}, f32[640,512]{1,0:T(8,128)}, f32[64,2,8,128]{3,2,1,0:T(8,128)}, bf16[512,5120]{1,0:T(8,128)(2,1)}) custom-call(s32[16]{0:T(128)S(1)} %stack.67.scalars, bf16[64,5120]{1,0:T(8,128)(2,1)S(1)} %copy-done.3, bf16[64,4096]{1,0:T(8,128)(2,1)S(1)} %copy-done.4, bf16[32,9216]{1,0:T(8,128)(2,1)S(1)} %collective-permute-done.refs_0_, ...), custom_call_target="tpu_custom_call" | custom-call | flops 6039797760 | bytes 24000000 | tf_op jit(solution)/shard_map/pallas_call | solution.py:370
  59.6 5.4 %all-to-all-start = ((f32[128,8,128]{2,1,0:T(8,128)}), f32[128,8,128]{2,1,0:T(8,128)S(1)}, u32[]{:S(2)}, u32[]{:S(2)}) async-start(f32[128,8,128]{2,1,0:T(8,128)} %bitcast.20), calls=%async_computation | async-start | bytes 1048576 | tf_op jit(solution)/shard_map/all_to_all | solution.py:397
  65.0 4.1 %shard_map.104 = (f32[1280,512]{1,0:T(8,128)}, f32[1280,512]{1,0:T(8,128)}) custom-call(f32[640,512]{1,0:T(8,128)} %copy-done.1, f32[640,512]{1,0:T(8,128)} %get-tuple-element.59.t_mine, f32[640,512]{1,0:T(8,128)} %collective-permute-done.14.s_theirs, f32[640,512]{1,0:T(8,128)} %collective-permute-done.15.t_theirs), custom_call_target="tpu_custom_call" | custom-call | bytes 11000000 | tf_op jit(solution)/shard_map/pallas_call | solution.py:398
  69.0 9.8 %all-to-all-done.every = f32[128,8,128]{2,1,0:T(8,128)S(1)} async-done(((f32[128,8,128]{2,1,0:T(8,128)}), f32[128,8,128]{2,1,0:T(8,128)S(1)}, u32[]{:S(2)}, u32[]{:S(2)}) %all-to-all-start) | async-done | bytes 524320 | tf_op jit(solution)/shard_map/all_to_all | solution.py:397
  81.3 9.8 %shard_map.106 = (bf16[32,2,16,1280]{3,2,1,0:T(8,128)(2,1)}, bf16[640,512]{1,0:T(8,128)(2,1)}) custom-call(s32[1]{0:T(128)} %bitcast.17.scalars, f32[8,128]{1,0:T(8,128)} %copy-done.5, f32[8,128]{1,0:T(8,128)} %copy-done.8, f32[1,512]{1,0:T(1,128)} %bitcast.28, f32[1280,512]{1,0:T(8,128)} %get-tuple-element.64.student, ...), custom_call_target="tpu_custom_call" | custom-call | flops 3355443200 | bytes 16000000 | tf_op jit(solution)/shard_map/pallas_call | solution.py:418
  91.1 4.9 %all-to-all-start.1 = ((bf16[64,16,1280]{2,1,0:T(8,128)(2,1)}), bf16[64,16,1280]{2,1,0:T(8,128)(2,1)S(1)}, u32[]{:S(2)}, u32[]{:S(2)}) async-start(bf16[64,16,1280]{2,1,0:T(8,128)(2,1)} %bitcast.27), calls=%async_computation.1 | async-start | bytes 5242880 | tf_op jit(solution)/shard_map/all_to_all | solution.py:442
  97.3 2.5 %copy-done = bf16[512,5120]{1,0:T(8,128)(2,1)S(1)} copy-done((bf16[512,5120]{1,0:T(8,128)(2,1)S(1)}, bf16[512,5120]{1,0:T(8,128)(2,1)}, u32[]{:S(2)}) %copy-start) | copy-done | bytes 5242904
  99.7 5.9 %shard_map.107 = bf16[640,5120]{1,0:T(8,128)(2,1)} custom-call(bf16[640,512]{1,0:T(8,128)(2,1)S(1)} %copy-done.2, bf16[512,5120]{1,0:T(8,128)(2,1)S(1)} %copy-done), custom_call_target="tpu_custom_call" | custom-call | flops 3355443200 | bytes 13000000 | tf_op jit(solution)/shard_map/pallas_call | solution.py:446
  105.7 24.1 %all-to-all-done.1.parts = bf16[64,16,1280]{2,1,0:T(8,128)(2,1)S(1)} async-done(((bf16[64,16,1280]{2,1,0:T(8,128)(2,1)}), bf16[64,16,1280]{2,1,0:T(8,128)(2,1)S(1)}, u32[]{:S(2)}, u32[]{:S(2)}) %all-to-all-start.1) | async-done | bytes 2621472 | tf_op jit(solution)/shard_map/all_to_all | solution.py:442
  130.1 13.0 %all_to_all.15.mine = bf16[8,16,1280]{2,1,0:T(8,128)(2,1)S(1)} all-to-all(bf16[8,16,1280]{2,1,0:T(8,128)(2,1)S(1)} %shard_map.108), channel_id=1, replica_groups={{0,2,4,6,8,10,12,14},{1,3,5,7,9,11,13,15},{16,18,20,22,24,26,28,30},{17..., dimensions={0} | all-to-all | bytes 655360 | tf_op jit(solution)/shard_map/all_to_all | solution.py:472
  143.1 2.4 %collective-permute-start.18 = (bf16[8,16,1280]{2,1,0:T(8,128)(2,1)S(1)}, bf16[8,16,1280]{2,1,0:T(8,128)(2,1)S(1)}, u32[]{:S(2)}, u32[]{:S(2)}) collective-permute-start(bf16[8,16,1280]{2,1,0:T(8,128)(2,1)S(1)} %all_to_all.15.mine), channel_id=1, source_target_pairs={{0,1},{1,0},{2,3},{3,2},{4,5},{5,4},{6,7},{7,6},{8,9},{9,8},{10,11... | collective-permute-start | bytes 983048 | tf_op jit(solution)/shard_map/ppermute | solution.py:48
  (57 shorter events, 14.4 us)
Async XLA Ops:
  2.6 13.5 %collective-permute-start = (bf16[32,9216]{1,0:T(8,128)(2,1)}, bf16[32,9216]{1,0:T(8,128)(2,1)S(1)}, u32[]{:S(2)}, u32[]{:S(2)}) collective-permute-start(bf16[32,9216]{1,0:T(8,128)(2,1)} %shard_map.102), channel_id=1, source_target_pairs={{0,16},{1,49},{2,18},{3,51},{4,20},{5,53},{6,22},{7,55},{8,24},{9,... | collective-permute-start | bytes 1769480 | tf_op jit(solution)/shard_map/ppermute | solution.py:48
  7.2 9.6 %collective-permute-start.1 = (bf16[32,9216]{1,0:T(8,128)(2,1)}, bf16[32,9216]{1,0:T(8,128)(2,1)S(1)}, u32[]{:S(2)}, u32[]{:S(2)}) collective-permute-start(bf16[32,9216]{1,0:T(8,128)(2,1)} %shard_map.102), channel_id=1, source_target_pairs={{0,64},{1,67},{2,66},{3,65},{4,68},{5,71},{6,70},{7,69},{8,72},{9,... | collective-permute-start | bytes 1769480 | tf_op jit(solution)/shard_map/ppermute | solution.py:48
  12.1 33.7 %copy-start.3 = (bf16[64,5120]{1,0:T(8,128)(2,1)S(1)}, bf16[64,5120]{1,0:T(8,128)(2,1)}, u32[]{:S(2)}) copy-start(bf16[64,5120]{1,0:T(8,128)(2,1)} %own_s.1) | copy-start | bytes 1966084
  12.1 33.7 %copy-start.4 = (bf16[64,4096]{1,0:T(8,128)(2,1)S(1)}, bf16[64,4096]{1,0:T(8,128)(2,1)}, u32[]{:S(2)}) copy-start(bf16[64,4096]{1,0:T(8,128)(2,1)} %own_t.1) | copy-start | bytes 1572868
  12.1 33.7 %copy-start.7 = (s32[512]{0:T(512)S(1)}, s32[512]{0:T(512)}, u32[]{:S(2)}) copy-start(s32[512]{0:T(512)} %param.11) | copy-start | bytes 6148
  16.9 9.8 %collective-permute-start.2 = (bf16[32,9216]{1,0:T(8,128)(2,1)S(1)}, bf16[32,9216]{1,0:T(8,128)(2,1)S(1)}, u32[]{:S(2)}, u32[]{:S(2)}) collective-permute-start(bf16[32,9216]{1,0:T(8,128)(2,1)S(1)} %collective-permute-done.refs_0_), channel_id=1, source_target_pairs={{0,64},{1,67},{2,66},{3,65},{4,68},{5,71},{6,70},{7,69},{8,72},{9,... | collective-permute-start | bytes 1769480 | tf_op jit(solution)/shard_map/ppermute | solution.py:48
  19.9 9.0 %collective-permute-start.3 = (bf16[32,9216]{1,0:T(8,128)(2,1)S(1)}, bf16[32,9216]{1,0:T(8,128)(2,1)S(1)}, u32[]{:S(2)}, u32[]{:S(2)}) collective-permute-start(bf16[32,9216]{1,0:T(8,128)(2,1)S(1)} %collective-permute-done.refs_0_), channel_id=1, source_target_pairs={{0,16},{1,49},{2,18},{3,51},{4,20},{5,53},{6,22},{7,55},{8,24},{9,... | collective-permute-start | bytes 1769480 | tf_op jit(solution)/shard_map/ppermute | solution.py:48
  20.0 9.6 %collective-permute-start.4 = (bf16[32,9216]{1,0:T(8,128)(2,1)S(1)}, bf16[32,9216]{1,0:T(8,128)(2,1)S(1)}, u32[]{:S(2)}, u32[]{:S(2)}) collective-permute-start(bf16[32,9216]{1,0:T(8,128)(2,1)S(1)} %collective-permute-done.refs_0_), channel_id=1, source_target_pairs={{0,4},{1,13},{2,6},{3,15},{4,8},{5,1},{6,10},{7,3},{8,12},{9,5},{1... | collective-permute-start | bytes 1769480 | tf_op jit(solution)/shard_map/ppermute | solution.py:48
  22.7 6.8 %collective-permute-start.5 = (bf16[32,9216]{1,0:T(8,128)(2,1)S(1)}, bf16[32,9216]{1,0:T(8,128)(2,1)S(1)}, u32[]{:S(2)}, u32[]{:S(2)}) collective-permute-start(bf16[32,9216]{1,0:T(8,128)(2,1)S(1)} %collective-permute-done.refs_0_), channel_id=1, source_target_pairs={{0,1},{1,0},{2,3},{3,2},{4,5},{5,4},{6,7},{7,6},{8,9},{9,8},{10,11... | collective-permute-start | bytes 1769480 | tf_op jit(solution)/shard_map/ppermute | solution.py:48
  22.7 6.8 %collective-permute-start.6 = (bf16[32,9216]{1,0:T(8,128)(2,1)S(1)}, bf16[32,9216]{1,0:T(8,128)(2,1)S(1)}, u32[]{:S(2)}, u32[]{:S(2)}) collective-permute-start(bf16[32,9216]{1,0:T(8,128)(2,1)S(1)} %collective-permute-done.1.refs_2_), channel_id=1, source_target_pairs={{0,1},{1,0},{2,3},{3,2},{4,5},{5,4},{6,7},{7,6},{8,9},{9,8},{10,11... | collective-permute-start | bytes 1769480 | tf_op jit(solution)/shard_map/ppermute | solution.py:48
  29.6 9.0 %collective-permute-start.7 = (bf16[32,9216]{1,0:T(8,128)(2,1)S(1)}, bf16[32,9216]{1,0:T(8,128)(2,1)S(1)}, u32[]{:S(2)}, u32[]{:S(2)}) collective-permute-start(bf16[32,9216]{1,0:T(8,128)(2,1)S(1)} %collective-permute-done.3.refs_3_), channel_id=1, source_target_pairs={{0,64},{1,67},{2,66},{3,65},{4,68},{5,71},{6,70},{7,69},{8,72},{9,... | collective-permute-start | bytes 1769480 | tf_op jit(solution)/shard_map/ppermute | solution.py:48
  30.2 8.4 %collective-permute-start.8 = (bf16[32,9216]{1,0:T(8,128)(2,1)S(1)}, bf16[32,9216]{1,0:T(8,128)(2,1)S(1)}, u32[]{:S(2)}, u32[]{:S(2)}) collective-permute-start(bf16[32,9216]{1,0:T(8,128)(2,1)S(1)} %collective-permute-done.2.refs_4_), channel_id=1, source_target_pairs={{0,1},{1,0},{2,3},{3,2},{4,5},{5,4},{6,7},{7,6},{8,9},{9,8},{10,11... | collective-permute-start | bytes 1769480 | tf_op jit(solution)/shard_map/ppermute | solution.py:48
  32.2 6.4 %collective-permute-start.9 = (bf16[32,9216]{1,0:T(8,128)(2,1)S(1)}, bf16[32,9216]{1,0:T(8,128)(2,1)S(1)}, u32[]{:S(2)}, u32[]{:S(2)}) collective-permute-start(bf16[32,9216]{1,0:T(8,128)(2,1)S(1)} %collective-permute-done.3.refs_3_), channel_id=1, source_target_pairs={{0,1},{1,0},{2,3},{3,2},{4,5},{5,4},{6,7},{7,6},{8,9},{9,8},{10,11... | collective-permute-start | bytes 1769480 | tf_op jit(solution)/shard_map/ppermute | solution.py:48
  32.2 9.7 %collective-permute-start.10 = (bf16[32,9216]{1,0:T(8,128)(2,1)S(1)}, bf16[32,9216]{1,0:T(8,128)(2,1)S(1)}, u32[]{:S(2)}, u32[]{:S(2)}) collective-permute-start(bf16[32,9216]{1,0:T(8,128)(2,1)S(1)} %collective-permute-done.2.refs_4_), channel_id=1, source_target_pairs={{0,4},{1,13},{2,6},{3,15},{4,8},{5,1},{6,10},{7,3},{8,12},{9,5},{1... | collective-permute-start | bytes 1769480 | tf_op jit(solution)/shard_map/ppermute | solution.py:48
  38.6 5.2 %collective-permute-start.11 = (bf16[32,9216]{1,0:T(8,128)(2,1)S(1)}, bf16[32,9216]{1,0:T(8,128)(2,1)S(1)}, u32[]{:S(2)}, u32[]{:S(2)}) collective-permute-start(bf16[32,9216]{1,0:T(8,128)(2,1)S(1)} %collective-permute-done.4.refs_1_), channel_id=1, source_target_pairs={{0,1},{1,0},{2,3},{3,2},{4,5},{5,4},{6,7},{7,6},{8,9},{9,8},{10,11... | collective-permute-start | bytes 1769480 | tf_op jit(solution)/shard_map/ppermute | solution.py:48
  41.8 2.5 %collective-permute-start.12 = (bf16[32,9216]{1,0:T(8,128)(2,1)S(1)}, bf16[32,9216]{1,0:T(8,128)(2,1)S(1)}, u32[]{:S(2)}, u32[]{:S(2)}) collective-permute-start(bf16[32,9216]{1,0:T(8,128)(2,1)S(1)} %collective-permute-done.7.refs_6_), channel_id=1, source_target_pairs={{0,1},{1,0},{2,3},{3,2},{4,5},{5,4},{6,7},{7,6},{8,9},{9,8},{10,11... | collective-permute-start | bytes 1769480 | tf_op jit(solution)/shard_map/ppermute | solution.py:48
  41.9 3.5 %collective-permute-start.13 = (bf16[32,9216]{1,0:T(8,128)(2,1)S(1)}, bf16[32,9216]{1,0:T(8,128)(2,1)S(1)}, u32[]{:S(2)}, u32[]{:S(2)}) collective-permute-start(bf16[32,9216]{1,0:T(8,128)(2,1)S(1)} %collective-permute-done.10.refs_5_), channel_id=1, source_target_pairs={{0,1},{1,0},{2,3},{3,2},{4,5},{5,4},{6,7},{7,6},{8,9},{9,8},{10,11... | collective-permute-start | bytes 1769480 | tf_op jit(solution)/shard_map/ppermute | solution.py:48
  45.4 35.3 %collective-permute-start.17 = (bf16[640,2560]{1,0:T(8,128)(2,1)}, bf16[640,2560]{1,0:T(8,128)(2,1)}, u32[]{:S(2)}, u32[]{:S(2)}) collective-permute-start(bf16[640,2560]{1,0:T(8,128)(2,1)} %constant_dynamic-slice_fusion), channel_id=1, source_target_pairs={{0,1},{1,0},{2,3},{3,2},{4,5},{5,4},{6,7},{7,6},{8,9},{9,8},{10,11... | collective-permute-start | bytes 9830408 | tf_op jit(solution)/shard_map/ppermute | solution.py:48
  58.5 6.4 %collective-permute-start.14 = (f32[640,512]{1,0:T(8,128)S(1)}, f32[640,512]{1,0:T(8,128)}, u32[]{:S(2)}, u32[]{:S(2)}) collective-permute-start(f32[640,512]{1,0:T(8,128)S(1)} %get-tuple-element.58.s_mine), channel_id=1, source_target_pairs={{0,1},{1,0},{2,3},{3,2},{4,5},{5,4},{6,7},{7,6},{8,9},{9,8},{10,11... | collective-permute-start | bytes 3932168 | tf_op jit(solution)/shard_map/ppermute | solution.py:48
  58.8 6.2 %collective-permute-start.15 = (f32[640,512]{1,0:T(8,128)}, f32[640,512]{1,0:T(8,128)}, u32[]{:S(2)}, u32[]{:S(2)}) collective-permute-start(f32[640,512]{1,0:T(8,128)} %get-tuple-element.59.t_mine), channel_id=1, source_target_pairs={{0,1},{1,0},{2,3},{3,2},{4,5},{5,4},{6,7},{7,6},{8,9},{9,8},{10,11... | collective-permute-start | bytes 3932168 | tf_op jit(solution)/shard_map/ppermute | solution.py:48
  59.6 19.2 %all-to-all-start = ((f32[128,8,128]{2,1,0:T(8,128)}), f32[128,8,128]{2,1,0:T(8,128)S(1)}, u32[]{:S(2)}, u32[]{:S(2)}) async-start(f32[128,8,128]{2,1,0:T(8,128)} %bitcast.20), calls=%async_computation | async-start | bytes 1048576 | tf_op jit(solution)/shard_map/all_to_all | solution.py:397
  79.2 1.5 %collective-permute-start.16 = (f32[8,128]{1,0:T(8,128)S(1)}, f32[8,128]{1,0:T(8,128)S(1)}, u32[]{:S(2)}, u32[]{:S(2)}) collective-permute-start(f32[8,128]{1,0:T(8,128)S(1)} %shard_map.105.mine), channel_id=1, source_target_pairs={{0,1},{1,0},{2,3},{3,2},{4,5},{5,4},{6,7},{7,6},{8,9},{9,8},{10,11... | collective-permute-start | bytes 12296 | tf_op jit(solution)/shard_map/ppermute | solution.py:48
  91.1 38.7 %all-to-all-start.1 = ((bf16[64,16,1280]{2,1,0:T(8,128)(2,1)}), bf16[64,16,1280]{2,1,0:T(8,128)(2,1)S(1)}, u32[]{:S(2)}, u32[]{:S(2)}) async-start(bf16[64,16,1280]{2,1,0:T(8,128)(2,1)} %bitcast.27), calls=%async_computation.1 | async-start | bytes 5242880 | tf_op jit(solution)/shard_map/all_to_all | solution.py:442
  143.1 3.7 %collective-permute-start.18 = (bf16[8,16,1280]{2,1,0:T(8,128)(2,1)S(1)}, bf16[8,16,1280]{2,1,0:T(8,128)(2,1)S(1)}, u32[]{:S(2)}, u32[]{:S(2)}) collective-permute-start(bf16[8,16,1280]{2,1,0:T(8,128)(2,1)S(1)} %all_to_all.15.mine), channel_id=1, source_target_pairs={{0,1},{1,0},{2,3},{3,2},{4,5},{5,4},{6,7},{7,6},{8,9},{9,8},{10,11... | collective-permute-start | bytes 983048 | tf_op jit(solution)/shard_map/ppermute | solution.py:48
  (7 other events, 21.6 us)
